TPU v7x, 128 devices: a whole 4x4x4 slice. The times are simulated.
128 devices in a mesh: row: 16 (over y, z_lo, core), col: 8 (over x, z_hi).
Axes of the slice: x: 4, y: 4, z: 4 (z_hi: 2, z_lo: 2; z = z_hi * 2 + z_lo), core: 2. Of those that a mesh axis runs over, the one named last changes fastest.
Arguments:
- base_quantized: bfloat16 [1536, 32768], P(('row', 'col')), may hold values from 0 to 4
- base_scales: float32 [1536, 256], P(('row', 'col')), may hold values from 0.08 to 15
- adjusted_quantized: bfloat16 [1536, 32768], P(('row', 'col')), may hold values from 0 to 5.6
- adjusted_scales: float32 [1536, 256], P(('row', 'col')), may hold values from 0.08 to 15
Outputs:
- correlation: bfloat16 [32768, 32768], P('row', 'col')
All inputs are finite; a program needn't handle non-finite values.
Results may differ from a plain program's by a relative error of at most 0.0034.
Values may be sent and summed in bfloat16 or wider, within the bound.
A program may use at most 128 MiB of HBM per device.

v0:
```python
import math

import jax
import jax.numpy as jnp
from jax import lax
from jax.sharding import PartitionSpec as P


def dequantize(quantized, scales):
    row_count = quantized.shape[0]
    grouped = (
        quantized.astype(jnp.float32).reshape(row_count, scales.shape[1], -1) * scales[:, :, None]
    )
    return grouped.reshape(row_count, -1)


def standardize(values, column_sum, squares, token_count):
    average = column_sum / token_count
    spread = squares / token_count - average * average
    scaled = (values - average) * lax.rsqrt(spread + 1e-06) * (1.0 / math.sqrt(token_count))
    return scaled.astype(jnp.bfloat16)


def contract_tokens(left, right):
    return lax.dot_general(
        left, right, (((0,), (0,)), ((), ())), preferred_element_type=jnp.float32
    )


def on_device(base_quantized, base_scales, adjusted_quantized, adjusted_scales):
    row_size = lax.axis_size("row")
    col_size = lax.axis_size("col")
    local_rows = base_quantized.shape[0]
    token_count = local_rows * row_size * col_size
    base_values = dequantize(base_quantized, base_scales)
    adjusted_values = dequantize(adjusted_quantized, adjusted_scales)
    moments = lax.psum(
        (
            jnp.sum(base_values, axis=0),
            jnp.sum(base_values * base_values, axis=0),
            jnp.sum(adjusted_values, axis=0),
            jnp.sum(adjusted_values * adjusted_values, axis=0),
        ),
        ("row", "col"),
    )
    base_unit = standardize(base_values, moments[0], moments[1], token_count)
    adjusted_unit = standardize(adjusted_values, moments[2], moments[3], token_count)
    base_rows = lax.all_to_all(base_unit, "row", split_axis=1, concat_axis=0, tiled=True)
    width_base = base_rows.shape[1]
    base_panel = lax.all_gather(base_rows, "col", axis=0, tiled=True)
    ordered = (
        base_panel.reshape(col_size, row_size, local_rows, width_base)
        .transpose(1, 0, 2, 3)
        .reshape(token_count, width_base)
    )
    adjusted_rows = lax.all_to_all(adjusted_unit, "col", split_axis=1, concat_axis=0, tiled=True)
    adjusted_panel = lax.all_gather(adjusted_rows, "row", axis=0, tiled=True)
    result = contract_tokens(ordered, adjusted_panel).astype(jnp.bfloat16)
    return result


def solution(mesh):
    in_specs = (
        P(("row", "col"), None),
        P(("row", "col"), None),
        P(("row", "col"), None),
        P(("row", "col"), None),
    )
    out_specs = P("row", "col")
    return jax.shard_map(
        on_device, mesh=mesh, in_specs=in_specs, out_specs=out_specs, check_vma=False
    )
```

profile of v0, /device:TPU:1, one launch (start us, length us, event | category | flops | bytes accessed | tf_op | source)
XLA Modules:
  0.0 396.7 jit_solution(908928736856091921)
XLA Ops:
  6.5 0.0 all-reduce.3.cloned.1.call-start
  6.5 1.2 mul.56
  7.7 0.2 pad
  7.9 0.0 copy-start.4
  7.9 1.2 copy.8
  9.1 0.0 copy-done.4
  9.1 0.0 copy-start
  9.2 0.5 mul.64
  9.6 0.2 pad.1
  9.8 0.0 copy-start.1
  9.8 1.2 copy.10
  11.1 0.0 copy-start.2
  11.1 0.0 copy-done
  11.1 0.0 copy-done.1
  11.1 1.5 fusion
  12.6 0.0 copy-done.2
  12.6 1.5 fusion.1
  14.1 0.0 all-reduce.3.cloned.1.call-update
  14.1 0.0 all-gather.3.cloned.1.call-start
  14.2 149.5 %all-reduce.3.cloned.1.call-done = (f32[32768]{0:T(1024)}, f32[32768]{0:T(1024)}, f32[32768]{0:T(1024)}, f32[32768]{0:T(1024)}) async-done(((f32[32768]{0:T(1024)}, f32[32768]{0:T(1024)}, f32[32768]{0:T(1024)}, f32[32768]{0:T(1024)}), (f32[32768]{0:T(1024)}, f32[32768]{0:T(1024)}, f32[32768]{0:T(1024)}, f32[32768]{0:T(1024)})) %all-reduce.3.cloned.1.call-update) | async-done | bytes 524304 | tf_op jit(solution)/shard_map/psum | solution.py:37
  163.7 1.2 broadcast_multiply_fusion
  164.9 2.0 multiply_convert_fusion.1
  166.9 0.6 copy.9
  167.5 0.1 slice
  167.6 0.5 copy.5
  168.0 0.0 copy-start.3
  168.0 19.5 %all_to_all.38 = bf16[12,16,2048]{2,0,1:T(8,128)(2,1)} all-to-all(bf16[12,16,2048]{2,0,1:T(8,128)(2,1)S(1)} %copy.5), channel_id=1, replica_groups=mesh['row'=16,'col'=8] {'row'}, dimensions={1} | all-to-all | bytes 1572864 | tf_op jit(solution)/shard_map/all_to_all | solution.py:48
  187.6 2.1 all_to_all.31
  189.7 0.0 all-gather.3.cloned.1.call-update
  189.7 0.0 all-gather.5.cloned.1.call-start
  189.7 0.0 copy-done.3
  189.7 0.4 multiply_convert_fusion
  190.1 0.6 copy.11
  190.7 0.1 slice.1
  190.8 0.5 copy.7
  191.2 24.6 %all_to_all.39 = bf16[12,8,4096]{2,0,1:T(8,128)(2,1)S(1)} all-to-all(bf16[12,8,4096]{2,0,1:T(8,128)(2,1)S(1)} %copy.7), channel_id=1, replica_groups=mesh['row'=16,'col'=8] {'col'}, dimensions={1} | all-to-all | bytes 1572864 | tf_op jit(solution)/shard_map/all_to_all | solution.py:56
  215.9 1.1 all_to_all.35
  216.9 0.0 all-gather.5.cloned.1.call-update
  217.0 67.9 %all-gather.3.cloned.1.call-done = bf16[1536,2048]{1,0:T(8,128)(2,1)} async-done(((bf16[192,2048]{1,0:T(8,128)(2,1)}), bf16[1536,2048]{1,0:T(8,128)(2,1)}) %all-gather.3.cloned.1.call-update) | async-done | bytes 6291472 | tf_op jit(solution)/shard_map/all_gather | solution.py:50
  284.9 10.6 %reshape.24 = bf16[8,16,12,2048]{3,2,1,0:T(8,128)(2,1)} reshape(bf16[1536,2048]{1,0:T(8,128)(2,1)} %all-gather.3.cloned.1.call-done) | data formatting | bytes 12582912 | tf_op jit(solution)/shard_map/reshape | solution.py:52
  295.5 8.2 %copy.6 = bf16[16,8,12,2048]{3,2,1,0:T(8,128)(2,1)} copy(bf16[16,8,12,2048]{3,2,0,1:T(8,128)(2,1)} %bitcast.17) | data formatting | bytes 12582912 | tf_op jit(solution)/shard_map/transpose | solution.py:53
  303.7 10.8 %reshape.25 = bf16[1536,2048]{1,0:T(8,128)(2,1)} reshape(bf16[16,8,12,2048]{3,2,1,0:T(8,128)(2,1)} %copy.6) | data formatting | bytes 12582912 | tf_op jit(solution)/shard_map/reshape | solution.py:54
  314.5 42.7 %all-gather.5.cloned.1.call-done = bf16[1536,4096]{1,0:T(8,128)(2,1)} async-done(((bf16[96,4096]{1,0:T(8,128)(2,1)}), bf16[1536,4096]{1,0:T(8,128)(2,1)}) %all-gather.5.cloned.1.call-update) | async-done | bytes 12582928 | tf_op jit(solution)/shard_map/all_gather | solution.py:57
  357.2 32.9 %convolution_convert_fusion = bf16[2048,4096]{1,0:T(8,128)(2,1)} fusion(bf16[1536,2048]{1,0:T(8,128)(2,1)} %reshape.25, bf16[1536,4096]{1,0:T(8,128)(2,1)} %all-gather.5.cloned.1.call-done), kind=kOutput, calls=%fused_computation | convolution fusion | flops 25778192384 | bytes 35651584 | tf_op jit(solution)/shard_map/dot_general | solution.py:25
Async XLA Ops:
  6.5 157.2 %all-reduce.3.cloned.1.call-start = ((), (), s32[]{:S(2)}) async-start(), calls=%async_computation.4 | async-start | bytes 1048576 | tf_op jit(solution)/shard_map/psum | solution.py:37
  7.9 1.2 copy-start.4
  9.1 1.9 copy-start
  9.8 1.3 copy-start.1
  11.1 1.5 copy-start.2
  14.1 270.8 %all-gather.3.cloned.1.call-start = ((), (), s32[]{:S(2)}) async-start(), calls=%async_computation.2 | async-start | bytes 7077888 | tf_op jit(solution)/shard_map/all_gather | solution.py:50
  168.0 21.7 %copy-start.3 = (bf16[12,32768]{1,0:T(8,128)(2,1)S(1)}, bf16[12,32768]{1,0:T(8,128)(2,1)}, u32[]{:S(2)}) copy-start(bf16[12,32768]{1,0:T(8,128)(2,1)} %param.6) | copy-start | bytes 2359300
  189.7 167.5 %all-gather.5.cloned.1.call-start = ((), (), s32[]{:S(2)}) async-start(), calls=%async_computation.3 | async-start | bytes 13369344 | tf_op jit(solution)/shard_map/all_gather | solution.py:57
Sparse Core Ops, SparseCore 0:
  14.2 149.4 all-reduce.2
  189.8 95.0 all-gather.2
  286.7 70.4 all-gather.4
where the time goes:
time: 398 us; the launch traced here: 397 us
  waiting for transfers between devices  260 us (65%)
  blocking collectives  44.2 us (11%)
  local copies, waits for them, and re-layouts  39.5 us (10%)
  matrix products  32.9 us (8%)
  between operations  13.3 us (3%)
  other arithmetic  6.54 us (2%)
    psum x1, waiting for transfers between devices, on_device(): lax.psum((jnp.sum(base_values, axis=0), jnp.sum(base_values * base_values...  150 us
    all_gather x1, waiting for transfers between devices, on_device(): base_panel = lax.all_gather(base_rows, 'col', axis=0, tiled=True)  67.9 us
    all_gather x1, waiting for transfers between devices, on_device(): adjusted_panel = lax.all_gather(adjusted_rows, 'row', axis=0, tiled=True)  42.7 us
    dot_general x1, matrix products, contract_tokens(): lax.dot_general(left, right, (((0,), (0,)), ((), ())), preferred_element_...  32.9 us
    all_to_all x1, blocking collectives, on_device(): lax.all_to_all(adjusted_unit, 'col', split_axis=1, concat_axis=0, tiled=T...  24.6 us
    all_to_all x1, blocking collectives, on_device(): lax.all_to_all(base_unit, 'row', split_axis=1, concat_axis=0, tiled=True)  19.5 us
    reshape x1, local copies, waits for them, and re-layouts, on_device(): ordered = base_panel.reshape(col_size, row_size, local_rows, width_base)....  10.8 us
    reshape x1, local copies, waits for them, and re-layouts, on_device(): base_panel.reshape(col_size, row_size, local_rows, width_base)  10.6 us
  transfers between devices with their start and end apart: 3, of which 3 were waited for; matrix products, arithmetic and copies ran while one was open for 8% of the time, Pallas kernels for 0%

commit v1 on v0

v1 whole, which is shorter than its diff:
```python
import functools
import math

import jax
import jax.numpy as jnp
from jax import lax
from jax.experimental import pallas as pl
from jax.experimental.pallas import tpu as pltpu
from jax.sharding import PartitionSpec as P

MESH = pl.DeviceIdType.MESH
VMEM = pltpu.VMEM
BF16 = jnp.bfloat16
F32 = jnp.float32

CORES = 2
RING = 4
GROUP = 128
SLOTS = RING * RING
OWNERS = 8
BASE, ADJ = 0, 1
CHUNK = 256
HALF = CHUNK // 2


def place():
    row, col = lax.axis_index("row"), lax.axis_index("col")
    x, z_hi = col // 2, col % 2
    y, z_lo, core = row // 4, (row // 2) % 2, row % 2
    return x, y, z_hi * 2 + z_lo, core


def device(x, y, z, core):
    x, y, z = x % RING, y % RING, z % RING
    return (y * 2 + z % 2) * CORES + core, x * 2 + z // 2


def gather_kernel(
    local, width,
    base_q, base_s, adj_q, adj_s,
    base_t, adj_u,
    peer_q, peer_s, send_q, send_s, raw, raw_s, unit,
    s0_send, s0_recv, s1_send, s1_recv, s2_send, s2_recv, s3_send, s3_recv,
    own_sem, swap_send, swap_recv,
):
    x, y, z, core = place()
    other = 1 - core
    chunks = width // CHUNK
    tokens = adj_u.shape[1]
    token_pair = 4 * local
    queue = (base_q, adj_q)
    scale = (base_s, adj_s)
    peer = device(x, y, z, other)

    def plane(op, slot):
        a, b = slot // RING, slot % RING
        return (x, y + a, z + b) if op == BASE else (x + a, y, z + b)

    def owner(op, slot):
        px, py, pz = plane(op, slot)
        if op == BASE:
            return (py % RING) * 2 + (pz % RING) % 2
        return (px % RING) * 2 + (pz % RING) // 2

    def along(op, step):
        return device(x + step, y, z, core) if op == BASE else device(x, y + step, z, core)

    def landing(op, i):
        return raw_s.at[op] if i == chunks else raw.at[i, op]

    def leaving(op, i):
        return send_s.at[op] if i == chunks else send_q.at[i, op]

    def remote(src, dst, send_sem, recv_sem, where):
        return pltpu.make_async_remote_copy(
            src_ref=src, dst_ref=dst, send_sem=send_sem, recv_sem=recv_sem,
            device_id=where, device_id_type=MESH,
        )

    def wait_for(ref, sem):
        pltpu.make_async_copy(ref, ref, sem).wait()

    barrier = pltpu.get_barrier_semaphore()
    greeted = [peer]
    for slot in range(1, SLOTS):
        greeted.append(device(*plane(BASE, slot), core))
        if slot >= RING:
            greeted.append(device(*plane(ADJ, slot), core))
    for where in greeted:
        pl.semaphore_signal(barrier, inc=1, device_id=where, device_id_type=MESH)
    pl.semaphore_wait(barrier, len(greeted))

    for op in (BASE, ADJ):
        for b in range(OWNERS):
            start = pl.multiple_of((2 * b + other) * width, width)
            remote(
                queue[op].at[:, pl.ds(start, width)], peer_q.at[op, b],
                s0_send.at[op], s0_recv.at[op], peer,
            ).start()
        remote(scale[op], peer_s.at[op], s0_send.at[2 + op], s0_recv.at[2 + op], peer).start()
    for op in (BASE, ADJ):
        wait_for(peer_q.at[op], s0_recv.at[op])
        wait_for(peer_s.at[op], s0_recv.at[2 + op])

    def both_cores(own, theirs):
        own, theirs = own.astype(F32), theirs.astype(F32)
        first = jnp.where(core == 0, own, theirs)
        second = jnp.where(core == 0, theirs, own)
        return jnp.concatenate([first, second], axis=0)

    lanes = lax.broadcasted_iota(jnp.int32, (8, 128), 1)
    per_block = width // GROUP
    subs = CORES * local // 8

    def pack_scales(op):
        all_s = both_cores(scale[op][...], peer_s[op])
        for b in range(OWNERS):
            tile = 2 * b * per_block // 128
            first = (2 * b * per_block) % 128
            packed = jnp.zeros((8, 128), F32)
            for sub in range(subs):
                part = all_s[sub * 8 : sub * 8 + 8, tile * 128 : tile * 128 + 128]
                shift = (sub * per_block + 256 - first - core * per_block) % 128
                part = pltpu.roll(part, shift, 1)
                mine = (lanes >= sub * per_block) & (lanes < (sub + 1) * per_block)
                packed = jnp.where(mine, part, packed)
            send_s[op, b] = packed

    def pack(op, i):
        @pl.loop(0, OWNERS)
        def _(b):
            parts = []
            for h in range(2):
                start = pl.multiple_of((2 * b + core) * width + i * CHUNK + h * HALF, HALF)
                parts.append(
                    both_cores(
                        queue[op][:, pl.ds(start, HALF)],
                        peer_q[op, b, :, pl.ds(i * CHUNK + h * HALF, HALF)],
                    )
                )
            send_q[i, op, b] = jnp.concatenate(parts, axis=0).astype(BF16)

    def scatter(op, i):
        for slot in range(1, SLOTS):
            remote(
                leaving(op, i).at[owner(op, slot)], landing(op, i).at[0, slot],
                s1_send.at[op, i], s1_recv.at[op, i], device(*plane(op, slot), core),
            ).start()
        pltpu.make_async_copy(
            leaving(op, i).at[owner(op, 0)], landing(op, i).at[0, 0], own_sem.at[op, i]
        ).start()

    def spread(op, i):
        wait_for(landing(op, i).at[0, pl.ds(1, SLOTS - 1)], s1_recv.at[op, i])
        wait_for(landing(op, i).at[0, 0], own_sem.at[op, i])
        for d, step in enumerate((1, -1)):
            remote(
                landing(op, i).at[0], landing(op, i).at[step % RING],
                s2_send.at[op, i, d], s2_recv.at[op, i, d], along(op, step),
            ).start()

    def forward(op, i):
        for d, step in enumerate((1, -1)):
            part = pl.ds(d * (SLOTS // 2), SLOTS // 2)
            wait_for(landing(op, i).at[step % RING], s2_recv.at[op, i, d])
            remote(
                landing(op, i).at[step % RING, part], landing(op, i).at[2, part],
                s3_send.at[op, i, d], s3_recv.at[op, i, d], along(op, step),
            ).start()

    def arrived(op, i):
        for d in range(2):
            part = pl.ds(d * (SLOTS // 2), SLOTS // 2)
            wait_for(landing(op, i).at[2, part], s3_recv.at[op, i, d])

    pairs = RING * SLOTS // 2

    def values(op, i, p):
        out = [[], []]
        for q in range(2):
            slot = (p % (SLOTS // 2)) * 2 + q
            block = raw[i, op, p // (SLOTS // 2), slot].astype(F32)
            s = raw_s[op, p // (SLOTS // 2), slot]
            for h in range(2):
                for sub in range(subs):
                    lane = sub * per_block + 2 * i + h
                    r = (h * subs + sub) * 8
                    out[h].append(block[r : r + 8] * s[:, lane : lane + 1])
        return out

    def standardize(op, i):
        def add(p, carry):
            sums, squares = carry
            parts = values(op, i, p)
            sums, squares = list(sums), list(squares)
            for h in range(2):
                for v in parts[h]:
                    sums[h] = sums[h] + v
                    squares[h] = squares[h] + v * v
            return tuple(sums), tuple(squares)

        zero = jnp.zeros((8, HALF), F32)
        sums, squares = lax.fori_loop(0, pairs, add, ((zero, zero), (zero, zero)))
        average, factor = [], []
        for h in range(2):
            a = jnp.sum(sums[h], axis=0, keepdims=True) / tokens
            spread_ = jnp.sum(squares[h], axis=0, keepdims=True) / tokens - a * a
            average.append(jnp.broadcast_to(a, (8, HALF)))
            factor.append(
                jnp.broadcast_to(lax.rsqrt(spread_ + 1e-06) * (1.0 / math.sqrt(tokens)), (8, HALF))
            )

        @pl.loop(0, pairs)
        def _(p):
            parts = values(op, i, p)
            for h in range(2):
                u = jnp.concatenate([(v - average[h]) * factor[h] for v in parts[h]], axis=0)
                column = i * CHUNK + h * HALF
                if op == BASE:
                    start = pl.multiple_of(p * token_pair, token_pair)
                    unit[pl.ds(start, token_pair), h * HALF : (h + 1) * HALF] = u.astype(BF16)
                else:
                    at = ((p % 8) // 2) * 8 + (p // 8) * 2 + p % 2
                    start = pl.multiple_of(at * token_pair, token_pair)
                    adj_u[core, pl.ds(start, token_pair), column : column + HALF] = u.astype(BF16)

    def finish(i):
        column = pl.ds(i * CHUNK, CHUNK)
        arrived(ADJ, i)
        standardize(ADJ, i)
        remote(
            adj_u.at[core, :, column], adj_u.at[core, :, column],
            swap_send.at[i], swap_recv.at[i], peer,
        ).start()
        arrived(BASE, i)
        standardize(BASE, i)

        @pl.loop(0, tokens // 128)
        def _(t):
            start = pl.multiple_of(t * 128, 128)
            base_t[column, pl.ds(start, 128)] = unit[pl.ds(start, 128), :].T

        wait_for(adj_u.at[other, :, column], swap_recv.at[i])

    for op in (BASE, ADJ):
        pack_scales(op)
        scatter(op, chunks)
    for step in range(chunks + 3):
        if step < chunks:
            for op in (BASE, ADJ):
                pack(op, step)
                scatter(op, step)
        i = step - 1
        if 0 <= i < chunks:
            for op in (BASE, ADJ):
                if i == 0:
                    spread(op, chunks)
                spread(op, i)
        i = step - 2
        if 0 <= i < chunks:
            for op in (BASE, ADJ):
                if i == 0:
                    forward(op, chunks)
                forward(op, i)
        i = step - 3
        if 0 <= i < chunks:
            if i == 0:
                arrived(BASE, chunks)
                arrived(ADJ, chunks)
            finish(i)

    for op in (BASE, ADJ):
        wait_for(peer_q.at[op], s0_send.at[op])
        wait_for(peer_s.at[op], s0_send.at[2 + op])
        for i in range(chunks + 1):
            wait_for(landing(op, i).at[0, pl.ds(1, SLOTS - 1)], s1_send.at[op, i])
            for d in range(2):
                wait_for(landing(op, i).at[0], s2_send.at[op, i, d])
                wait_for(landing(op, i).at[0, pl.ds(0, SLOTS // 2)], s3_send.at[op, i, d])
    for i in range(chunks):
        wait_for(adj_u.at[core, :, pl.ds(i * CHUNK, CHUNK)], swap_send.at[i])


def gather(base_q, base_s, adj_q, adj_s):
    local, latents = base_q.shape
    width = latents // (OWNERS * CORES)
    chunks = width // CHUNK
    tokens = local * CORES * RING**3
    rows = 2 * CORES * local
    dma = pltpu.SemaphoreType.DMA
    whole = pl.BlockSpec(memory_space=VMEM)
    return pl.pallas_call(
        functools.partial(gather_kernel, local, width),
        out_shape=(VMEM((width, tokens), BF16), VMEM((CORES, tokens, width), BF16)),
        in_specs=[whole] * 4,
        out_specs=(whole, whole),
        scratch_shapes=[
            VMEM((2, OWNERS, local, width), BF16),
            VMEM((2,) + base_s.shape, F32),
            VMEM((chunks, 2, OWNERS, rows, HALF), BF16),
            VMEM((2, OWNERS, 8, 128), F32),
            VMEM((chunks, 2, RING, SLOTS, rows, HALF), BF16),
            VMEM((2, RING, SLOTS, 8, 128), F32),
            VMEM((tokens, CHUNK), BF16),
            dma((4,)), dma((4,)),
            dma((2, chunks + 1)), dma((2, chunks + 1)),
            dma((2, chunks + 1, 2)), dma((2, chunks + 1, 2)),
            dma((2, chunks + 1, 2)), dma((2, chunks + 1, 2)),
            dma((2, chunks + 1)),
            dma((chunks,)), dma((chunks,)),
        ],
        compiler_params=pltpu.CompilerParams(
            collective_id=0, has_side_effects=True, vmem_limit_bytes=28 << 20
        ),
        name="gather_units",
    )(base_q, base_s, adj_q, adj_s)


TILE_M, TILE_N = 256, 512


def product_kernel(base_t, adj_u, out, stage, sems):
    width = base_t.shape[0]
    per_row = CORES * width // TILE_N
    tiles = (width // TILE_M) * per_row

    def target(t):
        r = pl.multiple_of((t // per_row) * TILE_M, TILE_M)
        c = pl.multiple_of((t % per_row) * TILE_N, TILE_N)
        return out.at[pl.ds(r, TILE_M), pl.ds(c, TILE_N)]

    def copy(t):
        return pltpu.make_async_copy(stage.at[t % 4], target(t), sems.at[t % 4])

    @pl.loop(0, tiles)
    def _(t):
        r = pl.multiple_of((t // per_row) * TILE_M, TILE_M)
        n = t % per_row
        c = pl.multiple_of((n % (per_row // CORES)) * TILE_N, TILE_N)

        @pl.when(t >= 4)
        def _():
            copy(t - 4).wait()

        stage[t % 4] = jnp.dot(
            base_t[pl.ds(r, TILE_M), :],
            adj_u[n // (per_row // CORES), :, pl.ds(c, TILE_N)],
            preferred_element_type=F32,
        ).astype(BF16)
        copy(t).start()

    for t in range(tiles - 4, tiles):
        copy(t).wait()


def product(base_t, adj_u):
    width = base_t.shape[0]
    whole = pl.BlockSpec(memory_space=VMEM)
    return pl.pallas_call(
        product_kernel,
        out_shape=jax.ShapeDtypeStruct((width, CORES * width), BF16),
        in_specs=[whole, whole],
        out_specs=pl.BlockSpec(memory_space=pl.ANY),
        scratch_shapes=[
            VMEM((4, TILE_M, TILE_N), BF16),
            pltpu.SemaphoreType.DMA((4,)),
        ],
        compiler_params=pltpu.CompilerParams(vmem_limit_bytes=8 << 20),
        name="correlate",
    )(base_t, adj_u)


def on_device(base_q, base_s, adj_q, adj_s):
    base_t, adj_u = gather(base_q, base_s, adj_q, adj_s)
    base_t = pltpu.with_memory_space_constraint(base_t, VMEM)
    adj_u = pltpu.with_memory_space_constraint(adj_u, VMEM)
    return product(base_t, adj_u)


def solution(mesh):
    spec = P(("row", "col"), None)
    return jax.shard_map(
        on_device, mesh=mesh, in_specs=(spec,) * 4, out_specs=P("row", "col"), check_vma=False
    )
```

time: 398 us -> 186 us (0.47)
  waiting for transfers between devices: 260 us -> 0 us
  Pallas kernels: 0 us -> 182 us
  blocking collectives: 44.2 us -> 0 us
  local copies, waits for them, and re-layouts: 39.5 us -> 3.88 us
  matrix products: 32.9 us -> 0 us
  between operations: 13.3 us -> 0.01 us
  other arithmetic: 6.54 us -> 0 us
    pallas_call x0 -> x2, Pallas kernels: none -> 182 us  [the longest x1 144 us: gather(): pl.pallas_call(functools.partial(gather_kernel, local, width), out_shape=...]
    psum x1 -> x0, waiting for transfers between devices: 150 us -> none  [on_device(): lax.psum((jnp.sum(base_values, axis=0), jnp.sum(base_values * base_values...]
    all_gather x2 -> x0, waiting for transfers between devices: 111 us -> none  [the longest x1 67.9 us: on_device(): base_panel = lax.all_gather(base_rows, 'col', axis=0, tiled=True)]
    all_to_all x2 -> x0, blocking collectives: 44.2 us -> none  [the longest x1 24.6 us: on_device(): lax.all_to_all(adjusted_unit, 'col', split_axis=1, concat_axis=0, tiled=T...]
    dot_general x1 -> x0, matrix products: 32.9 us -> none  [contract_tokens(): lax.dot_general(left, right, (((0,), (0,)), ((), ())), preferred_element_...]
    reshape x2 -> x0, local copies, waits for them, and re-layouts: 21.4 us -> none  [the longest x1 10.8 us: on_device(): ordered = base_panel.reshape(col_size, row_size, local_rows, width_base)....]
    transpose x1 -> x0, local copies, waits for them, and re-layouts: 8.25 us -> none  [on_device(): ordered = base_panel.reshape(col_size, row_size, local_rows, width_base)....]
    all_to_all x6 -> x0, local copies, waits for them, and re-layouts: 4.18 us -> none  [the longest x3 2.6 us: on_device(): lax.all_to_all(base_unit, 'row', split_axis=1, concat_axis=0, tiled=True)]
  transfers between devices with their start and end apart: 3 -> 0, of which waited for: 3 -> 0; matrix products, arithmetic and copies ran while one was open for 8% -> 0% of each run, Pallas kernels for 0% -> 0%
where the time goes in v1:
time: 186 us
  Pallas kernels  182 us (98%)
  local copies, waits for them, and re-layouts  3.88 us (2%)
    pallas_call x1, Pallas kernels, gather(): pl.pallas_call(functools.partial(gather_kernel, local, width), out_shape=...  144 us
    pallas_call x1, Pallas kernels, product(): pl.pallas_call(product_kernel, out_shape=jax.ShapeDtypeStruct((width, COR...  38.3 us
    unnamed x8, local copies, waits for them, and re-layouts  3.88 us

profile of v1, /device:TPU:1, one launch (start us, length us, event | category | flops | bytes accessed | tf_op | source)
XLA Modules:
  0.0 186.1 jit_solution(18876450354199327)
XLA Ops:
  0.0 0.0 copy-start
  0.0 1.2 copy-done
  1.2 0.0 copy-start.1
  1.2 1.2 copy-done.1
  2.5 0.0 copy-start.2
  2.5 0.7 copy-done.2
  3.2 0.0 copy-start.3
  3.2 0.7 copy-done.3
  3.9 143.8 %gather_units.1 = (bf16[2048,1536]{1,0:T(8,128)(2,1)S(1)}, bf16[2,1536,2048]{2,1,0:T(8,128)(2,1)S(1)}) custom-call(bf16[12,32768]{1,0:T(8,128)(2,1)S(1)} %copy-done, f32[12,256]{1,0:T(8,128)S(1)} %copy-done.2, bf16[12,32768]{1,0:T(8,128)(2,1)S(1)} %copy-done.1, f32[12,256]{1,0:T(8,128)S(1)} %copy-done.3), custom_call_target="tpu_custom_call" | custom-call | tf_op jit(solution)/shard_map/gather_units/pallas_call | solution.py:292
  147.7 38.3 %correlate.1 = bf16[2048,4096]{1,0:T(8,128)(2,1)} custom-call(bf16[2048,1536]{1,0:T(8,128)(2,1)S(1)} %get-tuple-element.7.base_t, bf16[2,1536,2048]{2,1,0:T(8,128)(2,1)S(1)} %get-tuple-element.8.adj_u), custom_call_target="tpu_custom_call" | custom-call | tf_op jit(solution)/shard_map/correlate/pallas_call | solution.py:359
Async XLA Ops:
  0.0 1.2 copy-start
  1.2 1.2 copy-start.1
  2.5 0.7 copy-start.2
  3.2 0.7 copy-start.3

commit v2 on v1

--- a/solution.py
+++ b/solution.py
@@ -35,19 +35,47 @@
     return (y * 2 + z % 2) * CORES + core, x * 2 + z // 2
 
 
+def pieces(n, most):
+    count = max(1, -(-n // most))
+    edges = [n // CHUNK * j // count * CHUNK for j in range(count + 1)]
+    return [(a, b - a) for a, b in zip(edges, edges[1:]) if b > a]
+
+
+def multiply(base_t, adj_u, below, beside, i, done=None):
+    last = done is not None
+    new = slice(i * CHUNK, (i + 1) * CHUNK)
+    into = slice(0, CHUNK) if last else new
+
+    @pl.loop(0, CORES)
+    def _(half):
+        for a, n in pieces((i + 1) * CHUNK, 1024):
+            below[half, a : a + n, into] = jnp.dot(
+                base_t[a : a + n, :], adj_u[half, :, new], preferred_element_type=F32
+            ).astype(BF16)
+        if last:
+            done(half, 0)
+        for a, n in pieces(i * CHUNK, 1024):
+            beside[half, into, a : a + n] = jnp.dot(
+                base_t[new, :], adj_u[half, :, a : a + n], preferred_element_type=F32
+            ).astype(BF16)
+        if last:
+            done(half, 1)
+
+
 def gather_kernel(
     local, width,
     base_q, base_s, adj_q, adj_s,
-    base_t, adj_u,
-    peer_q, peer_s, send_q, send_s, raw, raw_s, unit,
-    s0_send, s0_recv, s1_send, s1_recv, s2_send, s2_recv, s3_send, s3_recv,
+    base_t, adj_u, early,
+    own_q, own_s, peer_q, peer_s, send_q, send_s, raw, raw_s,
+    split_s, pick, wide_s, work,
+    load_sem, s0_send, s0_recv, s1_send, s1_recv, s2_send, s2_recv, s3_send, s3_recv,
     own_sem, swap_send, swap_recv,
 ):
     x, y, z, core = place()
     other = 1 - core
     chunks = width // CHUNK
     tokens = adj_u.shape[1]
-    token_pair = 4 * local
+    token_ring = CORES * RING * local
     queue = (base_q, adj_q)
     scale = (base_s, adj_s)
     peer = device(x, y, z, other)
@@ -79,6 +107,19 @@
 
     def wait_for(ref, sem):
         pltpu.make_async_copy(ref, ref, sem).wait()
+
+    loads = []
+    for op in (BASE, ADJ):
+        for b in range(OWNERS):
+            start = pl.multiple_of((2 * b + core) * width, width)
+            loads.append(
+                pltpu.make_async_copy(
+                    queue[op].at[:, pl.ds(start, width)], own_q.at[op, b], load_sem.at[op, b]
+                )
+            )
+        loads.append(pltpu.make_async_copy(scale[op], own_s.at[op], load_sem.at[op, OWNERS]))
+    for load in loads:
+        load.start()
 
     barrier = pltpu.get_barrier_semaphore()
     greeted = [peer]
@@ -98,6 +139,8 @@
                 s0_send.at[op], s0_recv.at[op], peer,
             ).start()
         remote(scale[op], peer_s.at[op], s0_send.at[2 + op], s0_recv.at[2 + op], peer).start()
+    for load in loads:
+        load.wait()
     for op in (BASE, ADJ):
         wait_for(peer_q.at[op], s0_recv.at[op])
         wait_for(peer_s.at[op], s0_recv.at[2 + op])
@@ -113,7 +156,7 @@
     subs = CORES * local // 8
 
     def pack_scales(op):
-        all_s = both_cores(scale[op][...], peer_s[op])
+        all_s = both_cores(own_s[op], peer_s[op])
         for b in range(OWNERS):
             tile = 2 * b * per_block // 128
             first = (2 * b * per_block) % 128
@@ -131,13 +174,8 @@
         def _(b):
             parts = []
             for h in range(2):
-                start = pl.multiple_of((2 * b + core) * width + i * CHUNK + h * HALF, HALF)
-                parts.append(
-                    both_cores(
-                        queue[op][:, pl.ds(start, HALF)],
-                        peer_q[op, b, :, pl.ds(i * CHUNK + h * HALF, HALF)],
-                    )
-                )
+                part = pl.ds(i * CHUNK + h * HALF, HALF)
+                parts.append(both_cores(own_q[op, b, :, part], peer_q[op, b, :, part]))
             send_q[i, op, b] = jnp.concatenate(parts, axis=0).astype(BF16)
 
     def scatter(op, i):
@@ -173,56 +211,84 @@
             part = pl.ds(d * (SLOTS // 2), SLOTS // 2)
             wait_for(landing(op, i).at[2, part], s3_recv.at[op, i, d])
 
-    pairs = RING * SLOTS // 2
-
-    def values(op, i, p):
-        out = [[], []]
-        for q in range(2):
-            slot = (p % (SLOTS // 2)) * 2 + q
-            block = raw[i, op, p // (SLOTS // 2), slot].astype(F32)
-            s = raw_s[op, p // (SLOTS // 2), slot]
+    terms = subs * per_block
+
+    def make_pick():
+        row = lax.broadcasted_iota(jnp.int32, (256, 128), 0)
+        for i in range(chunks):
             for h in range(2):
                 for sub in range(subs):
                     lane = sub * per_block + 2 * i + h
-                    r = (h * subs + sub) * 8
-                    out[h].append(block[r : r + 8] * s[:, lane : lane + 1])
-        return out
+                    one = (row == lane) | (row == terms + lane) | (row == 128 + lane)
+                    at = (h * subs + sub) * 128
+                    pick[i, :, at : at + 128] = jnp.where(one, 1.0, 0.0).astype(BF16)
+
+    def split_scales(op):
+        lane = lax.broadcasted_iota(jnp.int32, (RING * SLOTS * 8, 128), 1)
+        s = jnp.where(lane < terms, raw_s[op].reshape(RING * SLOTS * 8, 128), 0.0)
+        high = s.astype(BF16).astype(F32)
+        middle = (s - high).astype(BF16).astype(F32)
+        low = (s - high) - middle
+        split_s[op, :, :128] = (high + pltpu.roll(middle, terms, 1)).astype(BF16)
+        split_s[op, :, 128:] = low.astype(BF16)
 
     def standardize(op, i):
+        for n in range(0, wide_s.shape[1], 256):
+            wide_s[:, n : n + 256] = jnp.dot(
+                split_s[op], pick[i, :, n : n + 256], preferred_element_type=F32
+            )
+
         def add(p, carry):
-            sums, squares = carry
-            parts = values(op, i, p)
-            sums, squares = list(sums), list(squares)
+            sums, squares = list(carry[0]), list(carry[1])
+            at = p if op == BASE else (p % RING) * RING + p // RING
+            s = wide_s[pl.ds(pl.multiple_of(p * RING * 8, RING * 8), RING * 8), :]
+            parts = [[], []]
+            for q in range(RING):
+                block = raw[i, op, p // RING, (p % RING) * RING + q].astype(F32)
+                for h in range(2):
+                    for sub in range(subs):
+                        n = h * subs + sub
+                        parts[h].append(
+                            block[n * 8 : n * 8 + 8]
+                            * s[q * 8 : q * 8 + 8, n * 128 : n * 128 + 128]
+                        )
+            start = pl.multiple_of(at * token_ring, token_ring)
             for h in range(2):
-                for v in parts[h]:
-                    sums[h] = sums[h] + v
-                    squares[h] = squares[h] + v * v
+                work[pl.ds(start, token_ring), h * HALF : (h + 1) * HALF] = jnp.concatenate(
+                    parts[h], axis=0
+                )
+                v = parts[h]
+                w = [u * u for u in v]
+                while len(v) > 1:
+                    v = [sum(v[j : j + 2][1:], v[j]) for j in range(0, len(v), 2)]
+                    w = [sum(w[j : j + 2][1:], w[j]) for j in range(0, len(w), 2)]
+                sums[h] = sums[h] + v[0]
+                squares[h] = squares[h] + w[0]
             return tuple(sums), tuple(squares)
 
         zero = jnp.zeros((8, HALF), F32)
-        sums, squares = lax.fori_loop(0, pairs, add, ((zero, zero), (zero, zero)))
+        sums, squares = lax.fori_loop(
+            0, RING * RING, add, ((zero, zero), (zero, zero)), unroll=2
+        )
         average, factor = [], []
         for h in range(2):
             a = jnp.sum(sums[h], axis=0, keepdims=True) / tokens
             spread_ = jnp.sum(squares[h], axis=0, keepdims=True) / tokens - a * a
-            average.append(jnp.broadcast_to(a, (8, HALF)))
-            factor.append(
-                jnp.broadcast_to(lax.rsqrt(spread_ + 1e-06) * (1.0 / math.sqrt(tokens)), (8, HALF))
-            )
-
-        @pl.loop(0, pairs)
-        def _(p):
-            parts = values(op, i, p)
+            average.append(a)
+            factor.append(lax.rsqrt(spread_ + 1e-06) * (1.0 / math.sqrt(tokens)))
+
+        rows = 128 if op == BASE else 96
+
+        @pl.loop(0, tokens // rows, unroll=2)
+        def _(t):
+            part = pl.ds(pl.multiple_of(t * rows, rows), rows)
             for h in range(2):
-                u = jnp.concatenate([(v - average[h]) * factor[h] for v in parts[h]], axis=0)
-                column = i * CHUNK + h * HALF
+                u = (work[part, h * HALF : (h + 1) * HALF] - average[h]) * factor[h]
+                column = slice(i * CHUNK + h * HALF, i * CHUNK + (h + 1) * HALF)
                 if op == BASE:
-                    start = pl.multiple_of(p * token_pair, token_pair)
-                    unit[pl.ds(start, token_pair), h * HALF : (h + 1) * HALF] = u.astype(BF16)
+                    base_t[column, part] = u.astype(BF16).T
                 else:
-                    at = ((p % 8) // 2) * 8 + (p // 8) * 2 + p % 2
-                    start = pl.multiple_of(at * token_pair, token_pair)
-                    adj_u[core, pl.ds(start, token_pair), column : column + HALF] = u.astype(BF16)
+                    adj_u[core, part, column] = u.astype(BF16)
 
     def finish(i):
         column = pl.ds(i * CHUNK, CHUNK)
@@ -234,22 +300,20 @@
         ).start()
         arrived(BASE, i)
         standardize(BASE, i)
-
-        @pl.loop(0, tokens // 128)
-        def _(t):
-            start = pl.multiple_of(t * 128, 128)
-            base_t[column, pl.ds(start, 128)] = unit[pl.ds(start, 128), :].T
-
         wait_for(adj_u.at[other, :, column], swap_recv.at[i])
-
-    for op in (BASE, ADJ):
-        pack_scales(op)
-        scatter(op, chunks)
+        if i < chunks - 1:
+            multiply(base_t, adj_u, early, early, i)
+
     for step in range(chunks + 3):
         if step < chunks:
             for op in (BASE, ADJ):
                 pack(op, step)
                 scatter(op, step)
+        if step == 0:
+            for op in (BASE, ADJ):
+                pack_scales(op)
+                scatter(op, chunks)
+            make_pick()
         i = step - 1
         if 0 <= i < chunks:
             for op in (BASE, ADJ):
@@ -265,8 +329,9 @@
         i = step - 3
         if 0 <= i < chunks:
             if i == 0:
-                arrived(BASE, chunks)
-                arrived(ADJ, chunks)
+                for op in (BASE, ADJ):
+                    arrived(op, chunks)
+                    split_scales(op)
             finish(i)
 
     for op in (BASE, ADJ):
@@ -285,23 +350,35 @@
     local, latents = base_q.shape
     width = latents // (OWNERS * CORES)
     chunks = width // CHUNK
+    early = width - CHUNK
     tokens = local * CORES * RING**3
     rows = 2 * CORES * local
+    subs = CORES * local // 8
     dma = pltpu.SemaphoreType.DMA
     whole = pl.BlockSpec(memory_space=VMEM)
     return pl.pallas_call(
         functools.partial(gather_kernel, local, width),
-        out_shape=(VMEM((width, tokens), BF16), VMEM((CORES, tokens, width), BF16)),
-        in_specs=[whole] * 4,
-        out_specs=(whole, whole),
+        out_shape=(
+            VMEM((width, tokens), BF16),
+            VMEM((CORES, tokens, width), BF16),
+            VMEM((CORES, early, early), BF16),
+        ),
+        in_specs=[pl.BlockSpec(memory_space=pltpu.HBM)] * 4,
+        out_specs=(whole,) * 3,
         scratch_shapes=[
+            VMEM((2, OWNERS, local, width), BF16),
+            VMEM((2,) + base_s.shape, F32),
             VMEM((2, OWNERS, local, width), BF16),
             VMEM((2,) + base_s.shape, F32),
             VMEM((chunks, 2, OWNERS, rows, HALF), BF16),
             VMEM((2, OWNERS, 8, 128), F32),
             VMEM((chunks, 2, RING, SLOTS, rows, HALF), BF16),
             VMEM((2, RING, SLOTS, 8, 128), F32),
-            VMEM((tokens, CHUNK), BF16),
+            VMEM((2, RING * SLOTS * 8, 256), BF16),
+            VMEM((chunks, 256, 2 * subs * 128), BF16),
+            VMEM((RING * SLOTS * 8, 2 * subs * 128), F32),
+            VMEM((tokens, CHUNK), F32),
+            dma((2, OWNERS + 1)),
             dma((4,)), dma((4,)),
             dma((2, chunks + 1)), dma((2, chunks + 1)),
             dma((2, chunks + 1, 2)), dma((2, chunks + 1, 2)),
@@ -310,71 +387,68 @@
             dma((chunks,)), dma((chunks,)),
         ],
         compiler_params=pltpu.CompilerParams(
-            collective_id=0, has_side_effects=True, vmem_limit_bytes=28 << 20
+            collective_id=0, has_side_effects=True, vmem_limit_bytes=27 << 20
         ),
         name="gather_units",
     )(base_q, base_s, adj_q, adj_s)
 
 
-TILE_M, TILE_N = 256, 512
-
-
-def product_kernel(base_t, adj_u, out, stage, sems):
+def product_kernel(base_t, adj_u, early, out, below, beside, early_sem, late_sem):
     width = base_t.shape[0]
-    per_row = CORES * width // TILE_N
-    tiles = (width // TILE_M) * per_row
-
-    def target(t):
-        r = pl.multiple_of((t // per_row) * TILE_M, TILE_M)
-        c = pl.multiple_of((t % per_row) * TILE_N, TILE_N)
-        return out.at[pl.ds(r, TILE_M), pl.ds(c, TILE_N)]
-
-    def copy(t):
-        return pltpu.make_async_copy(stage.at[t % 4], target(t), sems.at[t % 4])
-
-    @pl.loop(0, tiles)
-    def _(t):
-        r = pl.multiple_of((t // per_row) * TILE_M, TILE_M)
-        n = t % per_row
-        c = pl.multiple_of((n % (per_row // CORES)) * TILE_N, TILE_N)
-
-        @pl.when(t >= 4)
-        def _():
-            copy(t - 4).wait()
-
-        stage[t % 4] = jnp.dot(
-            base_t[pl.ds(r, TILE_M), :],
-            adj_u[n // (per_row // CORES), :, pl.ds(c, TILE_N)],
-            preferred_element_type=F32,
-        ).astype(BF16)
-        copy(t).start()
-
-    for t in range(tiles - 4, tiles):
-        copy(t).wait()
-
-
-def product(base_t, adj_u):
+    done_to = early.shape[1]
+    moves = [
+        pltpu.make_async_copy(
+            early.at[half, a : a + CHUNK],
+            out.at[a : a + CHUNK, half * width : half * width + done_to],
+            early_sem.at[half, a // CHUNK],
+        )
+        for half in range(CORES)
+        for a in range(0, done_to, CHUNK)
+    ]
+    for move in moves:
+        move.start()
+
+    def late(half, which):
+        start = pl.multiple_of(half * width, width)
+        if which == 0:
+            at = out.at[:, pl.ds(start + done_to, CHUNK)]
+            return pltpu.make_async_copy(below.at[half], at, late_sem.at[half, 0])
+        at = out.at[pl.ds(done_to, CHUNK), pl.ds(start, done_to)]
+        return pltpu.make_async_copy(beside.at[half], at, late_sem.at[half, 1])
+
+    multiply(
+        base_t, adj_u, below, beside, done_to // CHUNK,
+        lambda half, which: late(half, which).start(),
+    )
+    for half in range(CORES):
+        for which in range(2):
+            late(half, which).wait()
+    for move in moves:
+        move.wait()
+
+
+def product(base_t, adj_u, early):
     width = base_t.shape[0]
     whole = pl.BlockSpec(memory_space=VMEM)
     return pl.pallas_call(
         product_kernel,
         out_shape=jax.ShapeDtypeStruct((width, CORES * width), BF16),
-        in_specs=[whole, whole],
+        in_specs=[whole] * 3,
         out_specs=pl.BlockSpec(memory_space=pl.ANY),
         scratch_shapes=[
-            VMEM((4, TILE_M, TILE_N), BF16),
-            pltpu.SemaphoreType.DMA((4,)),
+            VMEM((CORES, width, CHUNK), BF16),
+            VMEM((CORES, CHUNK, width - CHUNK), BF16),
+            pltpu.SemaphoreType.DMA((CORES, width // CHUNK - 1)),
+            pltpu.SemaphoreType.DMA((CORES, 2)),
         ],
         compiler_params=pltpu.CompilerParams(vmem_limit_bytes=8 << 20),
         name="correlate",
-    )(base_t, adj_u)
-
-
-def on_device(base_q, base_s, adj_q, adj_s):
-    base_t, adj_u = gather(base_q, base_s, adj_q, adj_s)
-    base_t = pltpu.with_memory_space_constraint(base_t, VMEM)
-    adj_u = pltpu.with_memory_space_constraint(adj_u, VMEM)
-    return product(base_t, adj_u)
+    )(base_t, adj_u, early)
+
+
+def on_device(*args):
+    units = gather(*args)
+    return product(*(pltpu.with_memory_space_constraint(u, VMEM) for u in units))
 
 
 def solution(mesh):

time: 186 us -> 113 us (0.61)
  Pallas kernels: 182 us -> 112 us
  local copies, waits for them, and re-layouts: 3.88 us -> 0 us
    pallas_call x1, Pallas kernels: 144 us -> 105 us  [gather(): pl.pallas_call(functools.partial(gather_kernel, local, width), out_shape=...]
    pallas_call x1, Pallas kernels: 38.3 us -> 7.68 us  [product(): pl.pallas_call(product_kernel, out_shape=jax.ShapeDtypeStruct((width, COR...]
    unnamed x8 -> x0, local copies, waits for them, and re-layouts: 3.88 us -> none
where the time goes in v2:
time: 113 us
  Pallas kernels  112 us (99%)
    pallas_call x1, Pallas kernels, gather(): pl.pallas_call(functools.partial(gather_kernel, local, width), out_shape=...  105 us
    pallas_call x1, Pallas kernels, product(): pl.pallas_call(product_kernel, out_shape=jax.ShapeDtypeStruct((width, COR...  7.68 us

profile of v2, /device:TPU:1, one launch (start us, length us, event | category | flops | bytes accessed | tf_op | source)
XLA Modules:
  0.0 112.6 jit_solution(3245884572706077514)
XLA Ops:
  0.0 104.8 %gather_units.1 = (bf16[2048,1536]{1,0:T(8,128)(2,1)S(1)}, bf16[2,1536,2048]{2,1,0:T(8,128)(2,1)S(1)}, bf16[2,1792,1792]{2,1,0:T(8,128)(2,1)S(1)}) custom-call(bf16[12,32768]{1,0:T(8,128)(2,1)} %base_q.1, f32[12,256]{1,0:T(8,128)} %base_s.1, bf16[12,32768]{1,0:T(8,128)(2,1)} %adj_q.1, f32[12,256]{1,0:T(8,128)} %adj_s.1), custom_call_target="tpu_custom_call" | custom-call | tf_op jit(solution)/shard_map/gather_units/pallas_call | solution.py:359
  104.8 7.7 %correlate.1 = bf16[2048,4096]{1,0:T(8,128)(2,1)} custom-call(bf16[2048,1536]{1,0:T(8,128)(2,1)S(1)} %get-tuple-element.8.base_t, bf16[2,1536,2048]{2,1,0:T(8,128)(2,1)S(1)} %get-tuple-element.9.adj_u, bf16[2,1792,1792]{2,1,0:T(8,128)(2,1)S(1)} %get-tuple-element.10.early), custom_call_target="tpu_custom_call" | custom-call | tf_op jit(solution)/shard_map/correlate/pallas_call | solution.py:433

commit v3 on v2

--- a/solution.py
+++ b/solution.py
@@ -16,8 +16,8 @@
 CORES = 2
 RING = 4
 GROUP = 128
-SLOTS = RING * RING
 OWNERS = 8
+CHIPS = RING * 2 * OWNERS
 BASE, ADJ = 0, 1
 CHUNK = 256
 HALF = CHUNK // 2
@@ -68,27 +68,33 @@
     base_t, adj_u, early,
     own_q, own_s, peer_q, peer_s, send_q, send_s, raw, raw_s,
     split_s, pick, wide_s, work,
-    load_sem, s0_send, s0_recv, s1_send, s1_recv, s2_send, s2_recv, s3_send, s3_recv,
+    load_sem, s0_send, s0_recv, s1_send, s1_recv, ex_send, ex_recv, s2_send, s2_recv, s3_send, s3_recv,
     own_sem, swap_send, swap_recv,
 ):
     x, y, z, core = place()
     other = 1 - core
     chunks = width // CHUNK
     tokens = adj_u.shape[1]
-    token_ring = CORES * RING * local
+    local_pair = CORES * local
     queue = (base_q, adj_q)
     scale = (base_s, adj_s)
     peer = device(x, y, z, other)
 
-    def plane(op, slot):
-        a, b = slot // RING, slot % RING
-        return (x, y + a, z + b) if op == BASE else (x + a, y, z + b)
+    near, far = z + 1 - 2 * (z % 2), z + 2
+
+    def group(op, slot):
+        step, across = slot // 2, slot % 2
+        if op == BASE:
+            return x, y + step, (near if across else z)
+        return x + step, y, (far if across else z)
 
     def owner(op, slot):
-        px, py, pz = plane(op, slot)
+        px, py, pz = group(op, slot)
         if op == BASE:
-            return (py % RING) * 2 + (pz % RING) % 2
+            return (py % RING) * 2 + pz % 2
         return (px % RING) * 2 + (pz % RING) // 2
+
+    partner = (device(x, y, far, core), device(x, y, near, core))
 
     def along(op, step):
         return device(x + step, y, z, core) if op == BASE else device(x, y + step, z, core)
@@ -123,10 +129,8 @@
 
     barrier = pltpu.get_barrier_semaphore()
     greeted = [peer]
-    for slot in range(1, SLOTS):
-        greeted.append(device(*plane(BASE, slot), core))
-        if slot >= RING:
-            greeted.append(device(*plane(ADJ, slot), core))
+    for slot in range(1, OWNERS):
+        greeted += [device(*group(op, slot), core) for op in (BASE, ADJ)]
     for where in greeted:
         pl.semaphore_signal(barrier, inc=1, device_id=where, device_id_type=MESH)
     pl.semaphore_wait(barrier, len(greeted))
@@ -179,18 +183,25 @@
             send_q[i, op, b] = jnp.concatenate(parts, axis=0).astype(BF16)
 
     def scatter(op, i):
-        for slot in range(1, SLOTS):
+        for slot in range(1, OWNERS):
             remote(
-                leaving(op, i).at[owner(op, slot)], landing(op, i).at[0, slot],
-                s1_send.at[op, i], s1_recv.at[op, i], device(*plane(op, slot), core),
+                leaving(op, i).at[owner(op, slot)], landing(op, i).at[0, 0, slot],
+                s1_send.at[op, i], s1_recv.at[op, i], device(*group(op, slot), core),
             ).start()
         pltpu.make_async_copy(
-            leaving(op, i).at[owner(op, 0)], landing(op, i).at[0, 0], own_sem.at[op, i]
+            leaving(op, i).at[owner(op, 0)], landing(op, i).at[0, 0, 0], own_sem.at[op, i]
         ).start()
 
+    def exchange(op, i):
+        wait_for(landing(op, i).at[0, 0, pl.ds(1, OWNERS - 1)], s1_recv.at[op, i])
+        wait_for(landing(op, i).at[0, 0, 0], own_sem.at[op, i])
+        remote(
+            landing(op, i).at[0, 0], landing(op, i).at[0, 1],
+            ex_send.at[op, i], ex_recv.at[op, i], partner[op],
+        ).start()
+
     def spread(op, i):
-        wait_for(landing(op, i).at[0, pl.ds(1, SLOTS - 1)], s1_recv.at[op, i])
-        wait_for(landing(op, i).at[0, 0], own_sem.at[op, i])
+        wait_for(landing(op, i).at[0, 1], ex_recv.at[op, i])
         for d, step in enumerate((1, -1)):
             remote(
                 landing(op, i).at[0], landing(op, i).at[step % RING],
@@ -199,17 +210,15 @@
 
     def forward(op, i):
         for d, step in enumerate((1, -1)):
-            part = pl.ds(d * (SLOTS // 2), SLOTS // 2)
             wait_for(landing(op, i).at[step % RING], s2_recv.at[op, i, d])
             remote(
-                landing(op, i).at[step % RING, part], landing(op, i).at[2, part],
+                landing(op, i).at[step % RING, d], landing(op, i).at[2, d],
                 s3_send.at[op, i, d], s3_recv.at[op, i, d], along(op, step),
             ).start()
 
     def arrived(op, i):
         for d in range(2):
-            part = pl.ds(d * (SLOTS // 2), SLOTS // 2)
-            wait_for(landing(op, i).at[2, part], s3_recv.at[op, i, d])
+            wait_for(landing(op, i).at[2, d], s3_recv.at[op, i, d])
 
     terms = subs * per_block
 
@@ -224,8 +233,8 @@
                     pick[i, :, at : at + 128] = jnp.where(one, 1.0, 0.0).astype(BF16)
 
     def split_scales(op):
-        lane = lax.broadcasted_iota(jnp.int32, (RING * SLOTS * 8, 128), 1)
-        s = jnp.where(lane < terms, raw_s[op].reshape(RING * SLOTS * 8, 128), 0.0)
+        lane = lax.broadcasted_iota(jnp.int32, (CHIPS * 8, 128), 1)
+        s = jnp.where(lane < terms, raw_s[op].reshape(CHIPS * 8, 128), 0.0)
         high = s.astype(BF16).astype(F32)
         middle = (s - high).astype(BF16).astype(F32)
         low = (s - high) - middle
@@ -240,23 +249,22 @@
 
         def add(p, carry):
             sums, squares = list(carry[0]), list(carry[1])
-            at = p if op == BASE else (p % RING) * RING + p // RING
-            s = wide_s[pl.ds(pl.multiple_of(p * RING * 8, RING * 8), RING * 8), :]
+            s = wide_s[pl.ds(pl.multiple_of(p * 32, 32), 32), :]
             parts = [[], []]
-            for q in range(RING):
-                block = raw[i, op, p // RING, (p % RING) * RING + q].astype(F32)
+            for q in range(4):
+                block = raw[i, op, p // 4, (p // 2) % 2, (p % 2) * 4 + q].astype(F32)
+                at = p * 4 + q
+                if op == ADJ:
+                    at = (p % 2) * 32 + (q // 2) * 16 + (q % 2) * 8 + p // 2
+                part = pl.ds(pl.multiple_of(at * local_pair, 8), local_pair)
                 for h in range(2):
-                    for sub in range(subs):
-                        n = h * subs + sub
-                        parts[h].append(
-                            block[n * 8 : n * 8 + 8]
-                            * s[q * 8 : q * 8 + 8, n * 128 : n * 128 + 128]
-                        )
-            start = pl.multiple_of(at * token_ring, token_ring)
+                    mine = [
+                        block[n * 8 : n * 8 + 8] * s[q * 8 : q * 8 + 8, n * 128 : n * 128 + 128]
+                        for n in range(h * subs, (h + 1) * subs)
+                    ]
+                    work[part, h * HALF : (h + 1) * HALF] = jnp.concatenate(mine, axis=0)
+                    parts[h] += mine
             for h in range(2):
-                work[pl.ds(start, token_ring), h * HALF : (h + 1) * HALF] = jnp.concatenate(
-                    parts[h], axis=0
-                )
                 v = parts[h]
                 w = [u * u for u in v]
                 while len(v) > 1:
@@ -268,7 +276,7 @@
 
         zero = jnp.zeros((8, HALF), F32)
         sums, squares = lax.fori_loop(
-            0, RING * RING, add, ((zero, zero), (zero, zero)), unroll=2
+            0, CHIPS // 4, add, ((zero, zero), (zero, zero)), unroll=2
         )
         average, factor = [], []
         for h in range(2):
@@ -300,48 +308,61 @@
         ).start()
         arrived(BASE, i)
         standardize(BASE, i)
-        wait_for(adj_u.at[other, :, column], swap_recv.at[i])
-        if i < chunks - 1:
-            multiply(base_t, adj_u, early, early, i)
-
-    for step in range(chunks + 3):
-        if step < chunks:
-            for op in (BASE, ADJ):
-                pack(op, step)
-                scatter(op, step)
-        if step == 0:
-            for op in (BASE, ADJ):
-                pack_scales(op)
-                scatter(op, chunks)
-            make_pick()
-        i = step - 1
+
+    def both(do, i):
         if 0 <= i < chunks:
             for op in (BASE, ADJ):
-                if i == 0:
-                    spread(op, chunks)
-                spread(op, i)
-        i = step - 2
-        if 0 <= i < chunks:
+                do(op, i)
+
+    def depart(op, i):
+        pack(op, i)
+        scatter(op, i)
+
+    both(depart, 0)
+    for op in (BASE, ADJ):
+        pack_scales(op)
+        scatter(op, chunks)
+    both(depart, 1)
+    both(exchange, 0)
+    for op in (BASE, ADJ):
+        exchange(op, chunks)
+    both(depart, 2)
+    both(spread, 0)
+    for op in (BASE, ADJ):
+        spread(op, chunks)
+    both(exchange, 1)
+    both(depart, 3)
+    make_pick()
+    both(spread, 1)
+    both(exchange, 2)
+    for i in range(chunks + 1):
+        both(forward, i)
+        if i == 0:
             for op in (BASE, ADJ):
-                if i == 0:
-                    forward(op, chunks)
-                forward(op, i)
-        i = step - 3
-        if 0 <= i < chunks:
-            if i == 0:
-                for op in (BASE, ADJ):
-                    arrived(op, chunks)
-                    split_scales(op)
-            finish(i)
+                forward(op, chunks)
+        if i == 1:
+            for op in (BASE, ADJ):
+                arrived(op, chunks)
+                split_scales(op)
+        if i:
+            finish(i - 1)
+        both(spread, i + 2)
+        both(exchange, i + 3)
+        both(depart, i + 4)
+        if i:
+            wait_for(adj_u.at[other, :, pl.ds((i - 1) * CHUNK, CHUNK)], swap_recv.at[i - 1])
+            if i < chunks:
+                multiply(base_t, adj_u, early, early, i - 1)
 
     for op in (BASE, ADJ):
         wait_for(peer_q.at[op], s0_send.at[op])
         wait_for(peer_s.at[op], s0_send.at[2 + op])
         for i in range(chunks + 1):
-            wait_for(landing(op, i).at[0, pl.ds(1, SLOTS - 1)], s1_send.at[op, i])
+            wait_for(landing(op, i).at[0, 0, pl.ds(1, OWNERS - 1)], s1_send.at[op, i])
+            wait_for(landing(op, i).at[0, 0], ex_send.at[op, i])
             for d in range(2):
                 wait_for(landing(op, i).at[0], s2_send.at[op, i, d])
-                wait_for(landing(op, i).at[0, pl.ds(0, SLOTS // 2)], s3_send.at[op, i, d])
+                wait_for(landing(op, i).at[0, 0], s3_send.at[op, i, d])
     for i in range(chunks):
         wait_for(adj_u.at[core, :, pl.ds(i * CHUNK, CHUNK)], swap_send.at[i])
 
@@ -372,14 +393,15 @@
             VMEM((2,) + base_s.shape, F32),
             VMEM((chunks, 2, OWNERS, rows, HALF), BF16),
             VMEM((2, OWNERS, 8, 128), F32),
-            VMEM((chunks, 2, RING, SLOTS, rows, HALF), BF16),
-            VMEM((2, RING, SLOTS, 8, 128), F32),
-            VMEM((2, RING * SLOTS * 8, 256), BF16),
+            VMEM((chunks, 2, RING, 2, OWNERS, rows, HALF), BF16),
+            VMEM((2, RING, 2, OWNERS, 8, 128), F32),
+            VMEM((2, CHIPS * 8, 256), BF16),
             VMEM((chunks, 256, 2 * subs * 128), BF16),
-            VMEM((RING * SLOTS * 8, 2 * subs * 128), F32),
+            VMEM((CHIPS * 8, 2 * subs * 128), F32),
             VMEM((tokens, CHUNK), F32),
             dma((2, OWNERS + 1)),
             dma((4,)), dma((4,)),
+            dma((2, chunks + 1)), dma((2, chunks + 1)),
             dma((2, chunks + 1)), dma((2, chunks + 1)),
             dma((2, chunks + 1, 2)), dma((2, chunks + 1, 2)),
             dma((2, chunks + 1, 2)), dma((2, chunks + 1, 2)),

time: 113 us -> 113 us (level)
  no operation moved by 1% of the time
where the time goes in v3:
time: 113 us
  Pallas kernels  113 us (100%)
    pallas_call x1, Pallas kernels, gather(): pl.pallas_call(functools.partial(gather_kernel, local, width), out_shape=...  105 us
    pallas_call x1, Pallas kernels, product(): pl.pallas_call(product_kernel, out_shape=jax.ShapeDtypeStruct((width, COR...  7.68 us

profile of v3, /device:TPU:1, one launch (start us, length us, event | category | flops | bytes accessed | tf_op | source)
XLA Modules:
  0.0 112.8 jit_solution(14757687552323003707)
XLA Ops:
  0.0 105.0 %gather_units.1 = (bf16[2048,1536]{1,0:T(8,128)(2,1)S(1)}, bf16[2,1536,2048]{2,1,0:T(8,128)(2,1)S(1)}, bf16[2,1792,1792]{2,1,0:T(8,128)(2,1)S(1)}) custom-call(bf16[12,32768]{1,0:T(8,128)(2,1)} %base_q.1, f32[12,256]{1,0:T(8,128)} %base_s.1, bf16[12,32768]{1,0:T(8,128)(2,1)} %adj_q.1, f32[12,256]{1,0:T(8,128)} %adj_s.1), custom_call_target="tpu_custom_call" | custom-call | tf_op jit(solution)/shard_map/gather_units/pallas_call | solution.py:380
  105.0 7.7 %correlate.1 = bf16[2048,4096]{1,0:T(8,128)(2,1)} custom-call(bf16[2048,1536]{1,0:T(8,128)(2,1)S(1)} %get-tuple-element.8.base_t, bf16[2,1536,2048]{2,1,0:T(8,128)(2,1)S(1)} %get-tuple-element.9.adj_u, bf16[2,1792,1792]{2,1,0:T(8,128)(2,1)S(1)} %get-tuple-element.10.early), custom_call_target="tpu_custom_call" | custom-call | tf_op jit(solution)/shard_map/correlate/pallas_call | solution.py:455

commit v4 on v3

--- a/solution.py
+++ b/solution.py
@@ -23,6 +23,37 @@
 HALF = CHUNK // 2
 
 
+ORDER = (
+    "d0A d8A d1B d8B",
+    "d0B d1A d3B d2A",
+    "pick e0A e8A e0B",
+    "e8B e1A e1B d7B",
+    "d2B d3A e2A d6B",
+    "d4A s0A s8A s0B",
+    "s8B s1A s1B e2B",
+    "f0A f8A e3A e3B",
+    "d4B f0B f8B d6A",
+    "s2A d5A e4A d5B",
+    "f1A f1B s2B t8B",
+    "t0B s3A s3B f2A",
+    "e4B t8A t0A e5A",
+    "d7A s4A f2B t1B",
+    "e5B e6A e6B t1A",
+    "s4B f3A t2A m0a",
+    "f3B s5A m1a t2B",
+    "m2b s5B f4A e7A",
+    "e7B m1b t3A s6A",
+    "f4B m2a t3B s6B",
+    "f5A m3a s7A t4A",
+    "m3b f5B s7B t4B",
+    "f6A m4a t5A f6B",
+    "m4b t5B f7A m5a",
+    "t6A f7B m5b t6B",
+    "m6b t7A m6a t7B",
+    "m0b",
+)
+
+
 def place():
     row, col = lax.axis_index("row"), lax.axis_index("col")
     x, z_hi = col // 2, col % 2
@@ -41,25 +72,20 @@
     return [(a, b - a) for a, b in zip(edges, edges[1:]) if b > a]
 
 
-def multiply(base_t, adj_u, below, beside, i, done=None):
-    last = done is not None
+def columns(base_t, adj_u, out, i, at, half):
     new = slice(i * CHUNK, (i + 1) * CHUNK)
-    into = slice(0, CHUNK) if last else new
-
-    @pl.loop(0, CORES)
-    def _(half):
-        for a, n in pieces((i + 1) * CHUNK, 1024):
-            below[half, a : a + n, into] = jnp.dot(
-                base_t[a : a + n, :], adj_u[half, :, new], preferred_element_type=F32
-            ).astype(BF16)
-        if last:
-            done(half, 0)
-        for a, n in pieces(i * CHUNK, 1024):
-            beside[half, into, a : a + n] = jnp.dot(
-                base_t[new, :], adj_u[half, :, a : a + n], preferred_element_type=F32
-            ).astype(BF16)
-        if last:
-            done(half, 1)
+    for a, n in pieces((i + 1) * CHUNK, 1024):
+        out[half, a : a + n, at : at + CHUNK] = jnp.dot(
+            base_t[a : a + n, :], adj_u[half, :, new], preferred_element_type=F32
+        ).astype(BF16)
+
+
+def rows(base_t, adj_u, out, i, at, half):
+    new = slice(i * CHUNK, (i + 1) * CHUNK)
+    for a, n in pieces(i * CHUNK, 1024):
+        out[half, at : at + CHUNK, a : a + n] = jnp.dot(
+            base_t[new, :], adj_u[half, :, a : a + n], preferred_element_type=F32
+        ).astype(BF16)
 
 
 def gather_kernel(
@@ -249,17 +275,17 @@
 
         def add(p, carry):
             sums, squares = list(carry[0]), list(carry[1])
-            s = wide_s[pl.ds(pl.multiple_of(p * 32, 32), 32), :]
             parts = [[], []]
-            for q in range(4):
-                block = raw[i, op, p // 4, (p // 2) % 2, (p % 2) * 4 + q].astype(F32)
-                at = p * 4 + q
+            for q in range(OWNERS):
+                block = raw[i, op, p // 2, p % 2, q].astype(F32)
+                at = p * OWNERS + q
                 if op == ADJ:
-                    at = (p % 2) * 32 + (q // 2) * 16 + (q % 2) * 8 + p // 2
+                    at = (q // 2) * 16 + (q % 2) * 8 + p
                 part = pl.ds(pl.multiple_of(at * local_pair, 8), local_pair)
+                s = pl.ds(pl.multiple_of((p * OWNERS + q) * 8, 8), 8)
                 for h in range(2):
                     mine = [
-                        block[n * 8 : n * 8 + 8] * s[q * 8 : q * 8 + 8, n * 128 : n * 128 + 128]
+                        block[n * 8 : n * 8 + 8] * wide_s[s, n * 128 : n * 128 + 128]
                         for n in range(h * subs, (h + 1) * subs)
                     ]
                     work[part, h * HALF : (h + 1) * HALF] = jnp.concatenate(mine, axis=0)
@@ -276,7 +302,7 @@
 
         zero = jnp.zeros((8, HALF), F32)
         sums, squares = lax.fori_loop(
-            0, CHIPS // 4, add, ((zero, zero), (zero, zero)), unroll=2
+            0, CHIPS // OWNERS, add, ((zero, zero), (zero, zero)), unroll=2
         )
         average, factor = [], []
         for h in range(2):
@@ -287,7 +313,7 @@
 
         rows = 128 if op == BASE else 96
 
-        @pl.loop(0, tokens // rows, unroll=2)
+        @pl.loop(0, tokens // rows, unroll=3 if op == BASE else 4)
         def _(t):
             part = pl.ds(pl.multiple_of(t * rows, rows), rows)
             for h in range(2):
@@ -298,61 +324,44 @@
                 else:
                     adj_u[core, part, column] = u.astype(BF16)
 
-    def finish(i):
-        column = pl.ds(i * CHUNK, CHUNK)
-        arrived(ADJ, i)
-        standardize(ADJ, i)
-        remote(
-            adj_u.at[core, :, column], adj_u.at[core, :, column],
-            swap_send.at[i], swap_recv.at[i], peer,
-        ).start()
-        arrived(BASE, i)
-        standardize(BASE, i)
-
-    def both(do, i):
-        if 0 <= i < chunks:
-            for op in (BASE, ADJ):
-                do(op, i)
+    swapped = set()
 
     def depart(op, i):
-        pack(op, i)
+        if i < chunks:
+            pack(op, i)
+        else:
+            pack_scales(op)
         scatter(op, i)
 
-    both(depart, 0)
-    for op in (BASE, ADJ):
-        pack_scales(op)
-        scatter(op, chunks)
-    both(depart, 1)
-    both(exchange, 0)
-    for op in (BASE, ADJ):
-        exchange(op, chunks)
-    both(depart, 2)
-    both(spread, 0)
-    for op in (BASE, ADJ):
-        spread(op, chunks)
-    both(exchange, 1)
-    both(depart, 3)
-    make_pick()
-    both(spread, 1)
-    both(exchange, 2)
-    for i in range(chunks + 1):
-        both(forward, i)
-        if i == 0:
-            for op in (BASE, ADJ):
-                forward(op, chunks)
-        if i == 1:
-            for op in (BASE, ADJ):
-                arrived(op, chunks)
-                split_scales(op)
-        if i:
-            finish(i - 1)
-        both(spread, i + 2)
-        both(exchange, i + 3)
-        both(depart, i + 4)
-        if i:
-            wait_for(adj_u.at[other, :, pl.ds((i - 1) * CHUNK, CHUNK)], swap_recv.at[i - 1])
-            if i < chunks:
-                multiply(base_t, adj_u, early, early, i - 1)
+    def settle(op, i):
+        arrived(op, i)
+        if i == chunks:
+            split_scales(op)
+            return
+        standardize(op, i)
+        if op == ADJ:
+            mine = adj_u.at[core, :, pl.ds(i * CHUNK, CHUNK)]
+            remote(mine, mine, swap_send.at[i], swap_recv.at[i], peer).start()
+
+    def multiply(part, i):
+        if i not in swapped:
+            swapped.add(i)
+            wait_for(adj_u.at[other, :, pl.ds(i * CHUNK, CHUNK)], swap_recv.at[i])
+
+        @pl.loop(0, CORES)
+        def _(half):
+            (columns, rows)[part](base_t, adj_u, early, i, i * CHUNK, half)
+
+    stage = {
+        "d": depart, "e": exchange, "s": spread, "f": forward, "t": settle, "m": multiply,
+    }
+    for word in " ".join(ORDER).split():
+        if word == "pick":
+            make_pick()
+        elif word != "m0b":
+            stage[word[0]]("BA".index(word[2]) if word[0] != "m" else "ab".index(word[2]), int(word[1]))
+    i = chunks - 1
+    wait_for(adj_u.at[other, :, pl.ds(i * CHUNK, CHUNK)], swap_recv.at[i])
 
     for op in (BASE, ADJ):
         wait_for(peer_q.at[op], s0_send.at[op])
@@ -438,10 +447,13 @@
         at = out.at[pl.ds(done_to, CHUNK), pl.ds(start, done_to)]
         return pltpu.make_async_copy(beside.at[half], at, late_sem.at[half, 1])
 
-    multiply(
-        base_t, adj_u, below, beside, done_to // CHUNK,
-        lambda half, which: late(half, which).start(),
-    )
+    @pl.loop(0, CORES)
+    def _(half):
+        columns(base_t, adj_u, below, done_to // CHUNK, 0, half)
+        late(half, 0).start()
+        rows(base_t, adj_u, beside, done_to // CHUNK, 0, half)
+        late(half, 1).start()
+
     for half in range(CORES):
         for which in range(2):
             late(half, which).wait()

time: 113 us -> 108 us (0.956)
  Pallas kernels: 113 us -> 107 us
    pallas_call x1, Pallas kernels: 105 us -> 99.6 us  [gather(): pl.pallas_call(functools.partial(gather_kernel, local, width), out_shape=...]
where the time goes in v4:
time: 108 us; the launch traced here: 107 us
  Pallas kernels  107 us (99%)
    pallas_call x1, Pallas kernels, gather(): pl.pallas_call(functools.partial(gather_kernel, local, width), out_shape=...  99.6 us
    pallas_call x1, Pallas kernels, product(): pl.pallas_call(product_kernel, out_shape=jax.ShapeDtypeStruct((width, COR...  7.68 us

profile of v4, /device:TPU:1, one launch (start us, length us, event | category | flops | bytes accessed | tf_op | source)
XLA Modules:
  0.0 107.5 jit_solution(15057848021927951290)
XLA Ops:
  0.0 99.6 %gather_units.1 = (bf16[2048,1536]{1,0:T(8,128)(2,1)S(1)}, bf16[2,1536,2048]{2,1,0:T(8,128)(2,1)S(1)}, bf16[2,1792,1792]{2,1,0:T(8,128)(2,1)S(1)}) custom-call(bf16[12,32768]{1,0:T(8,128)(2,1)} %base_q.1, f32[12,256]{1,0:T(8,128)} %base_s.1, bf16[12,32768]{1,0:T(8,128)(2,1)} %adj_q.1, f32[12,256]{1,0:T(8,128)} %adj_s.1), custom_call_target="tpu_custom_call" | custom-call | tf_op jit(solution)/shard_map/gather_units/pallas_call | solution.py:389
  99.6 7.7 %correlate.1 = bf16[2048,4096]{1,0:T(8,128)(2,1)} custom-call(bf16[2048,1536]{1,0:T(8,128)(2,1)S(1)} %get-tuple-element.8.base_t, bf16[2,1536,2048]{2,1,0:T(8,128)(2,1)S(1)} %get-tuple-element.9.adj_u, bf16[2,1792,1792]{2,1,0:T(8,128)(2,1)S(1)} %get-tuple-element.10.early), custom_call_target="tpu_custom_call" | custom-call | tf_op jit(solution)/shard_map/correlate/pallas_call | solution.py:467

commit v5 on v4

--- a/solution.py
+++ b/solution.py
@@ -21,36 +21,36 @@
 BASE, ADJ = 0, 1
 CHUNK = 256
 HALF = CHUNK // 2
+DIRECT = (0, 8)
 
 
 ORDER = (
-    "d0A d8A d1B d8B",
-    "d0B d1A d3B d2A",
-    "pick e0A e8A e0B",
-    "e8B e1A e1B d7B",
-    "d2B d3A e2A d6B",
-    "d4A s0A s8A s0B",
-    "s8B s1A s1B e2B",
-    "f0A f8A e3A e3B",
-    "d4B f0B f8B d6A",
-    "s2A d5A e4A d5B",
-    "f1A f1B s2B t8B",
-    "t0B s3A s3B f2A",
-    "e4B t8A t0A e5A",
-    "d7A s4A f2B t1B",
-    "e5B e6A e6B t1A",
-    "s4B f3A t2A m0a",
-    "f3B s5A m1a t2B",
-    "m2b s5B f4A e7A",
-    "e7B m1b t3A s6A",
-    "f4B m2a t3B s6B",
-    "f5A m3a s7A t4A",
-    "m3b f5B s7B t4B",
-    "f6A m4a t5A f6B",
-    "m4b t5B f7A m5a",
-    "t6A f7B m5b t6B",
-    "m6b t7A m6a t7B",
-    "m0b",
+    "d1A d1B d0A d0B",
+    "d8A d8B e1A d2B",
+    "e1B pick d4B d4A",
+    "s0A s8A d2A s0B",
+    "s8B s1A d3A d3B",
+    "e2B s1B f0A f8A",
+    "e2A d6B f0B f8B",
+    "e3A d5A f1A d5B",
+    "e3B e4A s2B e4B",
+    "d7B f1B d6A s2A",
+    "s3A d7A t8A t1A",
+    "t0A f2B e5A e5B",
+    "f2A s3B t8B t1B",
+    "t0B s4A s4B f3A",
+    "e6A m0a m1a t2A",
+    "e6B f3B e7B s5A",
+    "t2B s5B e7A f4A",
+    "m2b t3A s6A f4B",
+    "m1b t3B s6B m2a",
+    "m3a f5A t4A f5B",
+    "s7A m3b t4B s7B",
+    "m4a f6A f6B t5A",
+    "m4b t5B m5a f7A",
+    "f7B m0b t6A m5b",
+    "t6B m6a t7A m6b",
+    "t7B",
 )
 
 
@@ -92,7 +92,7 @@
     local, width,
     base_q, base_s, adj_q, adj_s,
     base_t, adj_u, early,
-    own_q, own_s, peer_q, peer_s, send_q, send_s, raw, raw_s,
+    own_q, own_s, peer_q, peer_s, send_q, send_s, raw, first_s, raw_s,
     split_s, pick, wide_s, work,
     load_sem, s0_send, s0_recv, s1_send, s1_recv, ex_send, ex_recv, s2_send, s2_recv, s3_send, s3_recv,
     own_sem, swap_send, swap_recv,
@@ -108,11 +108,11 @@
 
     near, far = z + 1 - 2 * (z % 2), z + 2
 
-    def group(op, slot):
+    def group(op, slot, side=0):
         step, across = slot // 2, slot % 2
         if op == BASE:
-            return x, y + step, (near if across else z)
-        return x + step, y, (far if across else z)
+            return x, y + step, (near if across else z) + 2 * side
+        return x + step, y, (far if across else z) + (near - z) * side
 
     def owner(op, slot):
         px, py, pz = group(op, slot)
@@ -125,8 +125,16 @@
     def along(op, step):
         return device(x + step, y, z, core) if op == BASE else device(x, y + step, z, core)
 
-    def landing(op, i):
-        return raw_s.at[op] if i == chunks else raw.at[i, op]
+    def inbox(op, i):
+        return first_s.at[op] if i == chunks else raw.at[i, op, 0]
+
+    def slab(op, i, step):
+        return raw_s.at[op, step % RING] if i == chunks else raw.at[i, op, step % RING]
+
+    def half(op, i, step, d):
+        if i == chunks:
+            return raw_s.at[op, step % RING, pl.ds(d * (OWNERS // 2), OWNERS // 2)]
+        return raw.at[i, op, step % RING, d]
 
     def leaving(op, i):
         return send_s.at[op] if i == chunks else send_q.at[i, op]
@@ -157,6 +165,7 @@
     greeted = [peer]
     for slot in range(1, OWNERS):
         greeted += [device(*group(op, slot), core) for op in (BASE, ADJ)]
+        greeted += [device(*group(op, slot, 1), core) for op in (BASE, ADJ)[: slot]]
     for where in greeted:
         pl.semaphore_signal(barrier, inc=1, device_id=where, device_id_type=MESH)
     pl.semaphore_wait(barrier, len(greeted))
@@ -171,9 +180,6 @@
         remote(scale[op], peer_s.at[op], s0_send.at[2 + op], s0_recv.at[2 + op], peer).start()
     for load in loads:
         load.wait()
-    for op in (BASE, ADJ):
-        wait_for(peer_q.at[op], s0_recv.at[op])
-        wait_for(peer_s.at[op], s0_recv.at[2 + op])
 
     def both_cores(own, theirs):
         own, theirs = own.astype(F32), theirs.astype(F32)
@@ -211,40 +217,57 @@
     def scatter(op, i):
         for slot in range(1, OWNERS):
             remote(
-                leaving(op, i).at[owner(op, slot)], landing(op, i).at[0, 0, slot],
+                leaving(op, i).at[owner(op, slot)], inbox(op, i).at[0, slot],
                 s1_send.at[op, i], s1_recv.at[op, i], device(*group(op, slot), core),
             ).start()
+        if i in DIRECT:
+            for slot in range(OWNERS):
+                remote(
+                    leaving(op, i).at[owner(op, slot)], inbox(op, i).at[1, slot],
+                    ex_send.at[op, i], ex_recv.at[op, i], device(*group(op, slot, 1), core),
+                ).start()
         pltpu.make_async_copy(
-            leaving(op, i).at[owner(op, 0)], landing(op, i).at[0, 0, 0], own_sem.at[op, i]
+            leaving(op, i).at[owner(op, 0)], inbox(op, i).at[0, 0], own_sem.at[op, i]
         ).start()
 
+    def gathered(op, i):
+        wait_for(inbox(op, i).at[0, pl.ds(1, OWNERS - 1)], s1_recv.at[op, i])
+        wait_for(inbox(op, i).at[0, 0], own_sem.at[op, i])
+
     def exchange(op, i):
-        wait_for(landing(op, i).at[0, 0, pl.ds(1, OWNERS - 1)], s1_recv.at[op, i])
-        wait_for(landing(op, i).at[0, 0, 0], own_sem.at[op, i])
-        remote(
-            landing(op, i).at[0, 0], landing(op, i).at[0, 1],
-            ex_send.at[op, i], ex_recv.at[op, i], partner[op],
-        ).start()
+        if i not in DIRECT:
+            gathered(op, i)
+            remote(
+                inbox(op, i).at[0], inbox(op, i).at[1],
+                ex_send.at[op, i], ex_recv.at[op, i], partner[op],
+            ).start()
 
     def spread(op, i):
-        wait_for(landing(op, i).at[0, 1], ex_recv.at[op, i])
+        if i in DIRECT:
+            gathered(op, i)
+        wait_for(inbox(op, i).at[1], ex_recv.at[op, i])
+        if i == chunks:
+            for slot in range(OWNERS):
+                raw_s[op, 0, slot] = first_s[op, 0, slot] + pltpu.roll(
+                    first_s[op, 1, slot], terms, 1
+                )
         for d, step in enumerate((1, -1)):
             remote(
-                landing(op, i).at[0], landing(op, i).at[step % RING],
+                slab(op, i, 0), slab(op, i, step),
                 s2_send.at[op, i, d], s2_recv.at[op, i, d], along(op, step),
             ).start()
 
     def forward(op, i):
         for d, step in enumerate((1, -1)):
-            wait_for(landing(op, i).at[step % RING], s2_recv.at[op, i, d])
+            wait_for(slab(op, i, step), s2_recv.at[op, i, d])
             remote(
-                landing(op, i).at[step % RING, d], landing(op, i).at[2, d],
+                half(op, i, step, d), half(op, i, 2, d),
                 s3_send.at[op, i, d], s3_recv.at[op, i, d], along(op, step),
             ).start()
 
     def arrived(op, i):
         for d in range(2):
-            wait_for(landing(op, i).at[2, d], s3_recv.at[op, i, d])
+            wait_for(half(op, i, 2, d), s3_recv.at[op, i, d])
 
     terms = subs * per_block
 
@@ -259,19 +282,32 @@
                     pick[i, :, at : at + 128] = jnp.where(one, 1.0, 0.0).astype(BF16)
 
     def split_scales(op):
-        lane = lax.broadcasted_iota(jnp.int32, (CHIPS * 8, 128), 1)
-        s = jnp.where(lane < terms, raw_s[op].reshape(CHIPS * 8, 128), 0.0)
-        high = s.astype(BF16).astype(F32)
-        middle = (s - high).astype(BF16).astype(F32)
-        low = (s - high) - middle
-        split_s[op, :, :128] = (high + pltpu.roll(middle, terms, 1)).astype(BF16)
-        split_s[op, :, 128:] = low.astype(BF16)
-
-    def standardize(op, i):
-        for n in range(0, wide_s.shape[1], 256):
-            wide_s[:, n : n + 256] = jnp.dot(
+        n = OWNERS * 8
+        lane = lax.broadcasted_iota(jnp.int32, (n, 128), 1)
+        for step in range(RING):
+            both_sides = raw_s[op, step].reshape(n, 128)
+            for side in range(2):
+                s = pltpu.roll(both_sides, 128 - terms, 1) if side else both_sides
+                s = jnp.where(lane < terms, s, 0.0)
+                high = s.astype(BF16).astype(F32)
+                middle = (s - high).astype(BF16).astype(F32)
+                low = (s - high) - middle
+                at = pl.ds((step * 2 + side) * n, n)
+                split_s[op, at, :128] = (high + pltpu.roll(middle, terms, 1)).astype(BF16)
+                split_s[op, at, 128:] = low.astype(BF16)
+
+    def expand(op, i):
+        for n in range(0, wide_s.shape[2], 256):
+            wide_s[wide(op, i), :, n : n + 256] = jnp.dot(
                 split_s[op], pick[i, :, n : n + 256], preferred_element_type=F32
             )
+
+    def wide(op, i):
+        return 1 + op if i == chunks - 1 else 0
+
+    def standardize(op, i):
+        if i < chunks - 1:
+            expand(op, i)
 
         def add(p, carry):
             sums, squares = list(carry[0]), list(carry[1])
@@ -285,7 +321,7 @@
                 s = pl.ds(pl.multiple_of((p * OWNERS + q) * 8, 8), 8)
                 for h in range(2):
                     mine = [
-                        block[n * 8 : n * 8 + 8] * wide_s[s, n * 128 : n * 128 + 128]
+                        block[n * 8 : n * 8 + 8] * wide_s[wide(op, i), s, n * 128 : n * 128 + 128]
                         for n in range(h * subs, (h + 1) * subs)
                     ]
                     work[part, h * HALF : (h + 1) * HALF] = jnp.concatenate(mine, axis=0)
@@ -326,7 +362,13 @@
 
     swapped = set()
 
+    traded = set()
+
     def depart(op, i):
+        if op not in traded:
+            traded.add(op)
+            wait_for(peer_q.at[op], s0_recv.at[op])
+            wait_for(peer_s.at[op], s0_recv.at[2 + op])
         if i < chunks:
             pack(op, i)
         else:
@@ -342,6 +384,8 @@
         if op == ADJ:
             mine = adj_u.at[core, :, pl.ds(i * CHUNK, CHUNK)]
             remote(mine, mine, swap_send.at[i], swap_recv.at[i], peer).start()
+        if i == 0:
+            expand(op, chunks - 1)
 
     def multiply(part, i):
         if i not in swapped:
@@ -367,11 +411,11 @@
         wait_for(peer_q.at[op], s0_send.at[op])
         wait_for(peer_s.at[op], s0_send.at[2 + op])
         for i in range(chunks + 1):
-            wait_for(landing(op, i).at[0, 0, pl.ds(1, OWNERS - 1)], s1_send.at[op, i])
-            wait_for(landing(op, i).at[0, 0], ex_send.at[op, i])
+            wait_for(inbox(op, i).at[0, pl.ds(1, OWNERS - 1)], s1_send.at[op, i])
+            wait_for(inbox(op, i).at[0], ex_send.at[op, i])
             for d in range(2):
-                wait_for(landing(op, i).at[0], s2_send.at[op, i, d])
-                wait_for(landing(op, i).at[0, 0], s3_send.at[op, i, d])
+                wait_for(slab(op, i, 0), s2_send.at[op, i, d])
+                wait_for(half(op, i, 0, 0), s3_send.at[op, i, d])
     for i in range(chunks):
         wait_for(adj_u.at[core, :, pl.ds(i * CHUNK, CHUNK)], swap_send.at[i])
 
@@ -403,10 +447,11 @@
             VMEM((chunks, 2, OWNERS, rows, HALF), BF16),
             VMEM((2, OWNERS, 8, 128), F32),
             VMEM((chunks, 2, RING, 2, OWNERS, rows, HALF), BF16),
-            VMEM((2, RING, 2, OWNERS, 8, 128), F32),
+            VMEM((2, 2, OWNERS, 8, 128), F32),
+            VMEM((2, RING, OWNERS, 8, 128), F32),
             VMEM((2, CHIPS * 8, 256), BF16),
             VMEM((chunks, 256, 2 * subs * 128), BF16),
-            VMEM((CHIPS * 8, 2 * subs * 128), F32),
+            VMEM((3, CHIPS * 8, 2 * subs * 128), F32),
             VMEM((tokens, CHUNK), F32),
             dma((2, OWNERS + 1)),
             dma((4,)), dma((4,)),
@@ -418,7 +463,7 @@
             dma((chunks,)), dma((chunks,)),
         ],
         compiler_params=pltpu.CompilerParams(
-            collective_id=0, has_side_effects=True, vmem_limit_bytes=27 << 20
+            collective_id=0, has_side_effects=True, vmem_limit_bytes=30 << 20
         ),
         name="gather_units",
     )(base_q, base_s, adj_q, adj_s)

time: 108 us -> 103 us (0.954)
  Pallas kernels: 107 us -> 103 us
    pallas_call x1, Pallas kernels: 99.6 us -> 95.4 us  [gather(): pl.pallas_call(functools.partial(gather_kernel, local, width), out_shape=...]
where the time goes in v5:
time: 103 us
  Pallas kernels  103 us (100%)
    pallas_call x1, Pallas kernels, gather(): pl.pallas_call(functools.partial(gather_kernel, local, width), out_shape=...  95.4 us
    pallas_call x1, Pallas kernels, product(): pl.pallas_call(product_kernel, out_shape=jax.ShapeDtypeStruct((width, COR...  7.68 us

profile of v5, /device:TPU:1, one launch (start us, length us, event | category | flops | bytes accessed | tf_op | source)
XLA Modules:
  0.0 103.2 jit_solution(4377530327977941647)
XLA Ops:
  0.0 95.4 %gather_units.1 = (bf16[2048,1536]{1,0:T(8,128)(2,1)S(1)}, bf16[2,1536,2048]{2,1,0:T(8,128)(2,1)S(1)}, bf16[2,1792,1792]{2,1,0:T(8,128)(2,1)S(1)}) custom-call(bf16[12,32768]{1,0:T(8,128)(2,1)} %base_q.1, f32[12,256]{1,0:T(8,128)} %base_s.1, bf16[12,32768]{1,0:T(8,128)(2,1)} %adj_q.1, f32[12,256]{1,0:T(8,128)} %adj_s.1), custom_call_target="tpu_custom_call" | custom-call | tf_op jit(solution)/shard_map/gather_units/pallas_call | solution.py:433
  95.4 7.7 %correlate.1 = bf16[2048,4096]{1,0:T(8,128)(2,1)} custom-call(bf16[2048,1536]{1,0:T(8,128)(2,1)S(1)} %get-tuple-element.8.base_t, bf16[2,1536,2048]{2,1,0:T(8,128)(2,1)S(1)} %get-tuple-element.9.adj_u, bf16[2,1792,1792]{2,1,0:T(8,128)(2,1)S(1)} %get-tuple-element.10.early), custom_call_target="tpu_custom_call" | custom-call | tf_op jit(solution)/shard_map/correlate/pallas_call | solution.py:512

commit v6 on v5

--- a/solution.py
+++ b/solution.py
@@ -25,33 +25,35 @@
 
 
 ORDER = (
-    "d1A d1B d0A d0B",
-    "d8A d8B e1A d2B",
-    "e1B pick d4B d4A",
-    "s0A s8A d2A s0B",
-    "s8B s1A d3A d3B",
-    "e2B s1B f0A f8A",
-    "e2A d6B f0B f8B",
-    "e3A d5A f1A d5B",
-    "e3B e4A s2B e4B",
-    "d7B f1B d6A s2A",
-    "s3A d7A t8A t1A",
-    "t0A f2B e5A e5B",
-    "f2A s3B t8B t1B",
-    "t0B s4A s4B f3A",
-    "e6A m0a m1a t2A",
-    "e6B f3B e7B s5A",
-    "t2B s5B e7A f4A",
-    "m2b t3A s6A f4B",
-    "m1b t3B s6B m2a",
-    "m3a f5A t4A f5B",
-    "s7A m3b t4B s7B",
-    "m4a f6A f6B t5A",
-    "m4b t5B m5a f7A",
-    "f7B m0b t6A m5b",
+    "d1B d1A d0A d2B",
+    "d8A d8B d0B e1A",
+    "pick e1B d4B d4A",
+    "s0A s8A d2A d3A",
+    "d3B s0B s8B s1A",
+    "s1B e2B f0A f8A",
+    "e2A d5B f0B f8B",
+    "d6B f1A e3A e3B",
+    "d5A e4A d7B s2B",
+    "s2A t8A t0A e4B",
+    "d6A f1B d7A t1A",
+    "s3A f2B s3B t8B",
+    "t0B m0a e5A f2A",
+    "s4A t1B f3A e5B",
+    "s4B t2B t2A e6A",
+    "m1a s5A e7A f3B",
+    "e6B e7B m2a s5B",
+    "f4A m1b t3A s6A",
+    "m2b f4B t3B m3a",
+    "f5A s6B s7A t4A",
+    "m3b f5B t4B m4a",
+    "f6A t5A s7B f6B",
+    "m4b t5B f7A m5b",
+    "t6A m0b m5a f7B",
     "t6B m6a t7A m6b",
     "t7B",
 )
+
+EARLY = 2
 
 
 def place():
@@ -303,10 +305,11 @@
             )
 
     def wide(op, i):
-        return 1 + op if i == chunks - 1 else 0
+        ahead = i - (chunks - EARLY)
+        return 1 + 2 * ahead + op if ahead >= 0 else 0
 
     def standardize(op, i):
-        if i < chunks - 1:
+        if i < chunks - EARLY:
             expand(op, i)
 
         def add(p, carry):
@@ -384,8 +387,8 @@
         if op == ADJ:
             mine = adj_u.at[core, :, pl.ds(i * CHUNK, CHUNK)]
             remote(mine, mine, swap_send.at[i], swap_recv.at[i], peer).start()
-        if i == 0:
-            expand(op, chunks - 1)
+        if i < EARLY:
+            expand(op, chunks - 1 - i)
 
     def multiply(part, i):
         if i not in swapped:
@@ -451,7 +454,7 @@
             VMEM((2, RING, OWNERS, 8, 128), F32),
             VMEM((2, CHIPS * 8, 256), BF16),
             VMEM((chunks, 256, 2 * subs * 128), BF16),
-            VMEM((3, CHIPS * 8, 2 * subs * 128), F32),
+            VMEM((1 + 2 * EARLY, CHIPS * 8, 2 * subs * 128), F32),
             VMEM((tokens, CHUNK), F32),
             dma((2, OWNERS + 1)),
             dma((4,)), dma((4,)),

time: 103 us -> 101 us (0.981)
  Pallas kernels: 103 us -> 101 us
    pallas_call x1, Pallas kernels: 95.4 us -> 93 us  [gather(): pl.pallas_call(functools.partial(gather_kernel, local, width), out_shape=...]
where the time goes in v6:
time: 101 us
  Pallas kernels  101 us (100%)
    pallas_call x1, Pallas kernels, gather(): pl.pallas_call(functools.partial(gather_kernel, local, width), out_shape=...  93 us
    pallas_call x1, Pallas kernels, product(): pl.pallas_call(product_kernel, out_shape=jax.ShapeDtypeStruct((width, COR...  7.68 us

profile of v6, /device:TPU:1, one launch (start us, length us, event | category | flops | bytes accessed | tf_op | source)
XLA Modules:
  0.0 100.9 jit_solution(18331151565821508413)
XLA Ops:
  0.0 93.0 %gather_units.1 = (bf16[2048,1536]{1,0:T(8,128)(2,1)S(1)}, bf16[2,1536,2048]{2,1,0:T(8,128)(2,1)S(1)}, bf16[2,1792,1792]{2,1,0:T(8,128)(2,1)S(1)}) custom-call(bf16[12,32768]{1,0:T(8,128)(2,1)} %base_q.1, f32[12,256]{1,0:T(8,128)} %base_s.1, bf16[12,32768]{1,0:T(8,128)(2,1)} %adj_q.1, f32[12,256]{1,0:T(8,128)} %adj_s.1), custom_call_target="tpu_custom_call" | custom-call | tf_op jit(solution)/shard_map/gather_units/pallas_call | solution.py:436
  93.0 7.7 %correlate.1 = bf16[2048,4096]{1,0:T(8,128)(2,1)} custom-call(bf16[2048,1536]{1,0:T(8,128)(2,1)S(1)} %get-tuple-element.8.base_t, bf16[2,1536,2048]{2,1,0:T(8,128)(2,1)S(1)} %get-tuple-element.9.adj_u, bf16[2,1792,1792]{2,1,0:T(8,128)(2,1)S(1)} %get-tuple-element.10.early), custom_call_target="tpu_custom_call" | custom-call | tf_op jit(solution)/shard_map/correlate/pallas_call | solution.py:515

commit v7 on v6

--- a/solution.py
+++ b/solution.py
@@ -29,31 +29,31 @@
     "d8A d8B d0B e1A",
     "pick e1B d4B d4A",
     "s0A s8A d2A d3A",
-    "d3B s0B s8B s1A",
-    "s1B e2B f0A f8A",
-    "e2A d5B f0B f8B",
-    "d6B f1A e3A e3B",
-    "d5A e4A d7B s2B",
-    "s2A t8A t0A e4B",
-    "d6A f1B d7A t1A",
-    "s3A f2B s3B t8B",
-    "t0B m0a e5A f2A",
-    "s4A t1B f3A e5B",
-    "s4B t2B t2A e6A",
-    "m1a s5A e7A f3B",
-    "e6B e7B m2a s5B",
-    "f4A m1b t3A s6A",
-    "m2b f4B t3B m3a",
-    "f5A s6B s7A t4A",
-    "m3b f5B t4B m4a",
-    "f6A t5A s7B f6B",
-    "m4b t5B f7A m5b",
-    "t6A m0b m5a f7B",
-    "t6B m6a t7A m6b",
+    "s0B s8B e2B d3B",
+    "s1A s1B f0A f8A",
+    "e2A d6B e3A f0B",
+    "f8B d7B f1A d5B",
+    "s2B d5A e3B s2A",
+    "f1B e4A t8B t0B",
+    "e4B t8A t0A s3A",
+    "d6A f2B t1A d7A",
+    "f2A m0a e5A s3B",
+    "e5B t1B s4A m1a",
+    "t2B s4B f3A m1b",
+    "t2A e6A e6B e7A",
+    "e7B s5A f3B m2a",
+    "f4A s5B t3A m2b",
+    "s6A f4B t3B s6B",
+    "m3a f5A s7A m0b",
+    "t4A m3b f5B t4B",
+    "s7B m4a t5A f6A",
+    "m4b f6B f7A t5B",
+    "m5b t6A m5a t6B",
+    "f7B m6a t7A m6b",
     "t7B",
 )
 
-EARLY = 2
+EARLY = 3
 
 
 def place():
@@ -466,7 +466,7 @@
             dma((chunks,)), dma((chunks,)),
         ],
         compiler_params=pltpu.CompilerParams(
-            collective_id=0, has_side_effects=True, vmem_limit_bytes=30 << 20
+            collective_id=0, has_side_effects=True, vmem_limit_bytes=32 << 20
         ),
         name="gather_units",
     )(base_q, base_s, adj_q, adj_s)

time: 101 us -> 101 us (level)
  no operation moved by 1% of the time
where the time goes in v7:
time: 101 us
  Pallas kernels  101 us (100%)
    pallas_call x1, Pallas kernels, gather(): pl.pallas_call(functools.partial(gather_kernel, local, width), out_shape=...  93.3 us
    pallas_call x1, Pallas kernels, product(): pl.pallas_call(product_kernel, out_shape=jax.ShapeDtypeStruct((width, COR...  7.68 us

profile of v7, /device:TPU:1, one launch (start us, length us, event | category | flops | bytes accessed | tf_op | source)
XLA Modules:
  0.0 101.1 jit_solution(10807537259328651167)
XLA Ops:
  0.0 93.3 %gather_units.1 = (bf16[2048,1536]{1,0:T(8,128)(2,1)S(1)}, bf16[2,1536,2048]{2,1,0:T(8,128)(2,1)S(1)}, bf16[2,1792,1792]{2,1,0:T(8,128)(2,1)S(1)}) custom-call(bf16[12,32768]{1,0:T(8,128)(2,1)} %base_q.1, f32[12,256]{1,0:T(8,128)} %base_s.1, bf16[12,32768]{1,0:T(8,128)(2,1)} %adj_q.1, f32[12,256]{1,0:T(8,128)} %adj_s.1), custom_call_target="tpu_custom_call" | custom-call | tf_op jit(solution)/shard_map/gather_units/pallas_call | solution.py:436
  93.3 7.7 %correlate.1 = bf16[2048,4096]{1,0:T(8,128)(2,1)} custom-call(bf16[2048,1536]{1,0:T(8,128)(2,1)S(1)} %get-tuple-element.8.base_t, bf16[2,1536,2048]{2,1,0:T(8,128)(2,1)S(1)} %get-tuple-element.9.adj_u, bf16[2,1792,1792]{2,1,0:T(8,128)(2,1)S(1)} %get-tuple-element.10.early), custom_call_target="tpu_custom_call" | custom-call | tf_op jit(solution)/shard_map/correlate/pallas_call | solution.py:515
